TPU v7x, 128 devices: a whole 4x4x4 slice. The times are simulated.
128 devices in a mesh: outer: 2 (over y_hi), inner: 64 (over y_lo, z, x, core).
Axes of the slice: x: 4, y: 4 (y_hi: 2, y_lo: 2; y = y_hi * 2 + y_lo), z: 4, core: 2. Of those that a mesh axis runs over, the one named last changes fastest.
Arguments:
- queries: bfloat16 [40960, 2048], P(('outer', 'inner')), may hold values from -300 to 300
- keys: bfloat16 [40960, 128], P(('outer', 'inner')), may hold values from -6 to 6
- values: bfloat16 [40960, 128], P(('outer', 'inner')), may hold values from -6 to 6
- doc_lengths: int32 [64], replicated, may hold values from 1 to 4800, 40960 in all
Outputs:
- attended: bfloat16 [40960, 2048], P(('outer', 'inner'))
Inputs may be any that keep to these rules, and one draw needn't show every extreme that they name: `doc_lengths`: the lengths sum to 40960; the longest document has exactly 4800 tokens.
All inputs are finite; a program needn't handle non-finite values.
Results may differ from a plain program's by a relative error of at most 0.0036.
Values may be sent and summed in bfloat16 or wider, within the bound.
No kernel may reach another device: no remote copies, remote signals or barrier semaphores. Data moves between devices by JAX's collectives and lax.ppermute only.
A program may use at most 64 MiB of HBM per device.

v0:
```python
import jax
import jax.numpy as jnp
from jax import lax
from jax.sharding import PartitionSpec as P

REACH = 16


def from_behind(block, axis, distance):
    devices = range(lax.axis_size(axis))
    route = [(i - distance, i) for i in devices if i - distance in devices]
    return lax.ppermute(block, axis, route)


def doc_index(positions, doc_lengths):
    ends = jnp.cumsum(doc_lengths)
    return jnp.sum((ends[None, :] <= positions[:, None]).astype(jnp.int32), axis=1)


def attend(queries, keys, values, query_pos, key_pos, doc_lengths):
    tok_rows = queries.shape[0]
    head_size = keys.shape[1]
    heads = queries.shape[1] // head_size
    rows = queries.reshape(tok_rows * heads, head_size)
    query_doc = doc_index(query_pos, doc_lengths)
    key_doc = doc_index(key_pos, doc_lengths)
    row_pos = jnp.repeat(query_pos, heads)
    row_doc = jnp.repeat(query_doc, heads)
    block = min(1024, tok_rows * heads)
    count = tok_rows * heads // block
    scale = 1.0 / head_size**0.5

    def one_block(index):
        start = index * block
        piece = lax.dynamic_slice_in_dim(rows, start, block, 0)
        pos_piece = lax.dynamic_slice_in_dim(row_pos, start, block, 0)
        doc_piece = lax.dynamic_slice_in_dim(row_doc, start, block, 0)
        scores = (
            lax.dot_general(
                piece, keys, (((1,), (1,)), ((), ())), preferred_element_type=jnp.float32
            )
            * scale
        )
        allowed = (
            (key_pos[None, :] <= pos_piece[:, None])
            & (key_pos[None, :] >= 0)
            & (key_doc[None, :] == doc_piece[:, None])
        )
        scores = jnp.where(allowed, scores, jnp.float32(-1e30))
        highest = jnp.max(scores, axis=1)
        probs = jnp.exp(scores - highest[:, None])
        total = jnp.sum(probs, axis=1)
        summed = jnp.dot(probs.astype(jnp.bfloat16), values, preferred_element_type=jnp.float32)
        return (summed / total[:, None]).astype(jnp.bfloat16)

    result = lax.map(one_block, jnp.arange(count, dtype=jnp.int32))
    return result.reshape(tok_rows, heads * head_size)


def shards(queries, keys, values, doc_lengths):
    tok_rows = keys.shape[0]
    head_size = keys.shape[1]
    device = lax.axis_index(("outer", "inner"))
    start = device * tok_rows
    own_pair = jnp.stack([keys, values])
    window = jnp.zeros((2, REACH, tok_rows, head_size), jnp.bfloat16)
    window = lax.dynamic_update_slice_in_dim(window, own_pair[:, None], REACH - 1, 1)

    def step(index, carry):
        current, window = carry
        current = from_behind(current, ("outer", "inner"), 1)
        slot = (REACH - 1 - index).astype(jnp.int32)
        window = lax.dynamic_update_slice_in_dim(window, current[:, None], slot, 1)
        return (current, window)

    current, window = lax.fori_loop(1, REACH, step, (own_pair, window))
    window = window.reshape(2, REACH * tok_rows, head_size)
    query_pos = start + jnp.arange(tok_rows, dtype=jnp.int32)
    key_pos = start - (REACH - 1) * tok_rows + jnp.arange(REACH * tok_rows, dtype=jnp.int32)
    return attend(queries, window[0], window[1], query_pos, key_pos, doc_lengths)


def solution(mesh):
    placed = (
        P(("outer", "inner"), None),
        P(("outer", "inner"), None),
        P(("outer", "inner"), None),
        P(),
    )
    return jax.shard_map(
        shards, mesh=mesh, in_specs=placed, out_specs=P(("outer", "inner"), None), check_vma=False
    )
```

profile of v0, /device:TPU:16, one launch (start us, length us, event | category | flops | bytes accessed | tf_op | source)
XLA Modules:
  0.0 281.0 jit_solution(17679348311198758326)
XLA Ops:
  0.0 0.7 copy.7
  1.3 0.8 convert_reduce_fusion
  2.2 0.7 reshape.61
  2.9 0.9 fusion.21
  4.5 163.8 %while.26 = (s32[]{:T(128)}, bf16[2,320,128]{2,1,0:T(8,128)(2,1)S(1)}, bf16[2,16,320,128]{3,2,0,1:T(8,128)(2,1)S(1)}, s32[]{:T(128)}, s32[]{:T(128)}, /*index=5*/s32[]{:T(128)}, s32[]{:T(128)}) while((s32[]{:T(128)}, bf16[2,320,128]{2,1,0:T(8,128)(2,1)S(1)}, bf16[2,16,320,128]{3,2,0,1:T(8,128)(2,1)S(1)}, s32[]{:T(128)}, s32[]{:T(128)}, ...), condition=%wide.region_3.4_spmd, body=%wide.region_2.0_spmd.sunk | while | flops 6 | bytes 1310887 | solution.py:76
  4.5 1.9 collective-permute-start
  6.4 8.9 %collective-permute-done = bf16[2,320,128]{2,1,0:T(8,128)(2,1)S(1)} collective-permute-done((bf16[2,320,128]{2,1,0:T(8,128)(2,1)S(1)}, bf16[2,320,128]{2,1,0:T(8,128)(2,1)S(1)}, u32[]{:S(2)}, u32[]{:S(2)}) %collective-permute-start) | collective-permute-done | bytes 163872 | tf_op jit(solution)/shard_map/while/body/eval_jaxpr/ppermute | solution.py:12
  15.4 1.9 collective-permute-start
  17.3 8.9 %collective-permute-done = bf16[2,320,128]{2,1,0:T(8,128)(2,1)S(1)} collective-permute-done((bf16[2,320,128]{2,1,0:T(8,128)(2,1)S(1)}, bf16[2,320,128]{2,1,0:T(8,128)(2,1)S(1)}, u32[]{:S(2)}, u32[]{:S(2)}) %collective-permute-start) | collective-permute-done | bytes 163872 | tf_op jit(solution)/shard_map/while/body/eval_jaxpr/ppermute | solution.py:12
  26.3 1.9 collective-permute-start
  28.3 8.9 %collective-permute-done = bf16[2,320,128]{2,1,0:T(8,128)(2,1)S(1)} collective-permute-done((bf16[2,320,128]{2,1,0:T(8,128)(2,1)S(1)}, bf16[2,320,128]{2,1,0:T(8,128)(2,1)S(1)}, u32[]{:S(2)}, u32[]{:S(2)}) %collective-permute-start) | collective-permute-done | bytes 163872 | tf_op jit(solution)/shard_map/while/body/eval_jaxpr/ppermute | solution.py:12
  37.2 1.9 collective-permute-start
  39.2 8.9 %collective-permute-done = bf16[2,320,128]{2,1,0:T(8,128)(2,1)S(1)} collective-permute-done((bf16[2,320,128]{2,1,0:T(8,128)(2,1)S(1)}, bf16[2,320,128]{2,1,0:T(8,128)(2,1)S(1)}, u32[]{:S(2)}, u32[]{:S(2)}) %collective-permute-start) | collective-permute-done | bytes 163872 | tf_op jit(solution)/shard_map/while/body/eval_jaxpr/ppermute | solution.py:12
  48.2 1.9 collective-permute-start
  50.1 8.9 %collective-permute-done = bf16[2,320,128]{2,1,0:T(8,128)(2,1)S(1)} collective-permute-done((bf16[2,320,128]{2,1,0:T(8,128)(2,1)S(1)}, bf16[2,320,128]{2,1,0:T(8,128)(2,1)S(1)}, u32[]{:S(2)}, u32[]{:S(2)}) %collective-permute-start) | collective-permute-done | bytes 163872 | tf_op jit(solution)/shard_map/while/body/eval_jaxpr/ppermute | solution.py:12
  59.1 1.9 collective-permute-start
  61.0 8.9 %collective-permute-done = bf16[2,320,128]{2,1,0:T(8,128)(2,1)S(1)} collective-permute-done((bf16[2,320,128]{2,1,0:T(8,128)(2,1)S(1)}, bf16[2,320,128]{2,1,0:T(8,128)(2,1)S(1)}, u32[]{:S(2)}, u32[]{:S(2)}) %collective-permute-start) | collective-permute-done | bytes 163872 | tf_op jit(solution)/shard_map/while/body/eval_jaxpr/ppermute | solution.py:12
  70.0 1.9 collective-permute-start
  71.9 8.9 %collective-permute-done = bf16[2,320,128]{2,1,0:T(8,128)(2,1)S(1)} collective-permute-done((bf16[2,320,128]{2,1,0:T(8,128)(2,1)S(1)}, bf16[2,320,128]{2,1,0:T(8,128)(2,1)S(1)}, u32[]{:S(2)}, u32[]{:S(2)}) %collective-permute-start) | collective-permute-done | bytes 163872 | tf_op jit(solution)/shard_map/while/body/eval_jaxpr/ppermute | solution.py:12
  80.9 1.9 collective-permute-start
  82.9 8.9 %collective-permute-done = bf16[2,320,128]{2,1,0:T(8,128)(2,1)S(1)} collective-permute-done((bf16[2,320,128]{2,1,0:T(8,128)(2,1)S(1)}, bf16[2,320,128]{2,1,0:T(8,128)(2,1)S(1)}, u32[]{:S(2)}, u32[]{:S(2)}) %collective-permute-start) | collective-permute-done | bytes 163872 | tf_op jit(solution)/shard_map/while/body/eval_jaxpr/ppermute | solution.py:12
  91.8 1.9 collective-permute-start
  93.8 8.9 %collective-permute-done = bf16[2,320,128]{2,1,0:T(8,128)(2,1)S(1)} collective-permute-done((bf16[2,320,128]{2,1,0:T(8,128)(2,1)S(1)}, bf16[2,320,128]{2,1,0:T(8,128)(2,1)S(1)}, u32[]{:S(2)}, u32[]{:S(2)}) %collective-permute-start) | collective-permute-done | bytes 163872 | tf_op jit(solution)/shard_map/while/body/eval_jaxpr/ppermute | solution.py:12
  102.8 1.9 collective-permute-start
  104.7 8.9 %collective-permute-done = bf16[2,320,128]{2,1,0:T(8,128)(2,1)S(1)} collective-permute-done((bf16[2,320,128]{2,1,0:T(8,128)(2,1)S(1)}, bf16[2,320,128]{2,1,0:T(8,128)(2,1)S(1)}, u32[]{:S(2)}, u32[]{:S(2)}) %collective-permute-start) | collective-permute-done | bytes 163872 | tf_op jit(solution)/shard_map/while/body/eval_jaxpr/ppermute | solution.py:12
  113.7 1.9 collective-permute-start
  115.6 8.9 %collective-permute-done = bf16[2,320,128]{2,1,0:T(8,128)(2,1)S(1)} collective-permute-done((bf16[2,320,128]{2,1,0:T(8,128)(2,1)S(1)}, bf16[2,320,128]{2,1,0:T(8,128)(2,1)S(1)}, u32[]{:S(2)}, u32[]{:S(2)}) %collective-permute-start) | collective-permute-done | bytes 163872 | tf_op jit(solution)/shard_map/while/body/eval_jaxpr/ppermute | solution.py:12
  124.6 1.9 collective-permute-start
  126.5 8.9 %collective-permute-done = bf16[2,320,128]{2,1,0:T(8,128)(2,1)S(1)} collective-permute-done((bf16[2,320,128]{2,1,0:T(8,128)(2,1)S(1)}, bf16[2,320,128]{2,1,0:T(8,128)(2,1)S(1)}, u32[]{:S(2)}, u32[]{:S(2)}) %collective-permute-start) | collective-permute-done | bytes 163872 | tf_op jit(solution)/shard_map/while/body/eval_jaxpr/ppermute | solution.py:12
  135.5 1.9 collective-permute-start
  137.5 8.9 %collective-permute-done = bf16[2,320,128]{2,1,0:T(8,128)(2,1)S(1)} collective-permute-done((bf16[2,320,128]{2,1,0:T(8,128)(2,1)S(1)}, bf16[2,320,128]{2,1,0:T(8,128)(2,1)S(1)}, u32[]{:S(2)}, u32[]{:S(2)}) %collective-permute-start) | collective-permute-done | bytes 163872 | tf_op jit(solution)/shard_map/while/body/eval_jaxpr/ppermute | solution.py:12
  146.4 1.9 collective-permute-start
  148.4 8.9 %collective-permute-done = bf16[2,320,128]{2,1,0:T(8,128)(2,1)S(1)} collective-permute-done((bf16[2,320,128]{2,1,0:T(8,128)(2,1)S(1)}, bf16[2,320,128]{2,1,0:T(8,128)(2,1)S(1)}, u32[]{:S(2)}, u32[]{:S(2)}) %collective-permute-start) | collective-permute-done | bytes 163872 | tf_op jit(solution)/shard_map/while/body/eval_jaxpr/ppermute | solution.py:12
  157.4 1.9 collective-permute-start
  159.3 8.9 %collective-permute-done = bf16[2,320,128]{2,1,0:T(8,128)(2,1)S(1)} collective-permute-done((bf16[2,320,128]{2,1,0:T(8,128)(2,1)S(1)}, bf16[2,320,128]{2,1,0:T(8,128)(2,1)S(1)}, u32[]{:S(2)}, u32[]{:S(2)}) %collective-permute-start) | collective-permute-done | bytes 163872 | tf_op jit(solution)/shard_map/while/body/eval_jaxpr/ppermute | solution.py:12
  168.3 1.7 fusion.23
  170.0 3.3 %reshape.65 = bf16[5120,128]{1,0:T(8,128)(2,1)} reshape(bf16[320,2048]{1,0:T(8,128)(2,1)} %param.8) | data formatting | bytes 2621440 | tf_op jit(solution)/shard_map/reshape | solution.py:24
  173.3 104.5 %while.27 = (s32[]{:T(128)}, bf16[5,1024,128]{2,1,0:T(8,128)(2,1)}, s32[5]{0:T(128)S(1)}, s32[5120]{0:T(1024)}, s32[5120]{0:T(1024)}, /*index=5*/s32[5120]{0:T(1...) while((s32[]{:T(128)}, bf16[5,1024,128]{2,1,0:T(8,128)(2,1)}, ...), condition=%wide.region_8.9_spmd.clone, body=%wide.region_5.8_spmd.clone.sunk | while | flops 2742301696 | bytes 66177744 | solution.py:56
  173.3 0.6 dynamic_slice.26
  174.5 0.7 dynamic_slice.28
  175.2 8.6 %fusion.35 = (f32[1024]{0:T(1024)S(1)}, f32[1024,5120]{1,0:T(8,128)S(1)}) fusion(bf16[5120,128]{1,0:T(8,128)(2,1)} %get-tuple-element.318, bf16[5120,128]{1,0:T(8,128)(2,1)} %get-tuple-element.317, s32[]{:T(128)S(6)} %select_n.22, s32[1024]{0:T(1024)S(1)} %dynamic_slice.27, s32[5120]{0:T(1024)} %get-tuple-element.315, ...), kind=kOutput, calls=%fused_computation.22.clone.1 | convolution fusion | flops 1378876416 | bytes 22602756 | tf_op jit(solution)/shard_map/while/body/eval_jaxpr/dot_general | solution.py:39
  183.8 4.8 %fusion.36 = f32[1024]{0:T(1024)S(1)} fusion(f32[1024,5120]{1,0:T(8,128)S(1)} %get-tuple-element.260, f32[1024]{0:T(1024)S(1)} %get-tuple-element.261), kind=kLoop, calls=%fused_computation.4.clone.1 | loop fusion | flops 10484736 | bytes 20979712 | tf_op jit(solution)/shard_map/while/body/eval_jaxpr/reduce_sum | solution.py:52
  188.7 5.5 %fusion.37 = bf16[5,1024,128]{2,1,0:T(8,128)(2,1)} fusion(bf16[5,1024,128]{2,1,0:T(8,128)(2,1)} %get-tuple-element.298, s32[]{:T(128)} %get-tuple-element.297, bf16[5120,128]{1,0:T(8,128)(2,1)} %get-tuple-element.319, f32[1024,5120]{1,0:T(8,128)S(1)} %get-tuple-element.260, f32[1024]{0:T(1024)S(1)} %get-tuple-element.261, f32[1024]{0:T(1024)S(1)} %fusion.36), kind=kOutput, calls=%fused_computation.11.clone.1 | convolution fusion | flops 1352925184 | bytes 22553088 | tf_op jit(solution)/shard_map/while/body/eval_jaxpr/dot_general | solution.py:53
  194.2 0.6 dynamic_slice.26
  195.4 0.7 dynamic_slice.28
  196.1 8.6 %fusion.35 = (f32[1024]{0:T(1024)S(1)}, f32[1024,5120]{1,0:T(8,128)S(1)}) fusion(bf16[5120,128]{1,0:T(8,128)(2,1)} %get-tuple-element.318, bf16[5120,128]{1,0:T(8,128)(2,1)} %get-tuple-element.317, s32[]{:T(128)S(6)} %select_n.22, s32[1024]{0:T(1024)S(1)} %dynamic_slice.27, s32[5120]{0:T(1024)} %get-tuple-element.315, ...), kind=kOutput, calls=%fused_computation.22.clone.1 | convolution fusion | flops 1378876416 | bytes 22602756 | tf_op jit(solution)/shard_map/while/body/eval_jaxpr/dot_general | solution.py:39
  204.7 4.8 %fusion.36 = f32[1024]{0:T(1024)S(1)} fusion(f32[1024,5120]{1,0:T(8,128)S(1)} %get-tuple-element.260, f32[1024]{0:T(1024)S(1)} %get-tuple-element.261), kind=kLoop, calls=%fused_computation.4.clone.1 | loop fusion | flops 10484736 | bytes 20979712 | tf_op jit(solution)/shard_map/while/body/eval_jaxpr/reduce_sum | solution.py:52
  209.6 5.5 %fusion.37 = bf16[5,1024,128]{2,1,0:T(8,128)(2,1)} fusion(bf16[5,1024,128]{2,1,0:T(8,128)(2,1)} %get-tuple-element.298, s32[]{:T(128)} %get-tuple-element.297, bf16[5120,128]{1,0:T(8,128)(2,1)} %get-tuple-element.319, f32[1024,5120]{1,0:T(8,128)S(1)} %get-tuple-element.260, f32[1024]{0:T(1024)S(1)} %get-tuple-element.261, f32[1024]{0:T(1024)S(1)} %fusion.36), kind=kOutput, calls=%fused_computation.11.clone.1 | convolution fusion | flops 1352925184 | bytes 22553088 | tf_op jit(solution)/shard_map/while/body/eval_jaxpr/dot_general | solution.py:53
  215.1 0.6 dynamic_slice.26
  216.3 0.7 dynamic_slice.28
  217.0 8.6 %fusion.35 = (f32[1024]{0:T(1024)S(1)}, f32[1024,5120]{1,0:T(8,128)S(1)}) fusion(bf16[5120,128]{1,0:T(8,128)(2,1)} %get-tuple-element.318, bf16[5120,128]{1,0:T(8,128)(2,1)} %get-tuple-element.317, s32[]{:T(128)S(6)} %select_n.22, s32[1024]{0:T(1024)S(1)} %dynamic_slice.27, s32[5120]{0:T(1024)} %get-tuple-element.315, ...), kind=kOutput, calls=%fused_computation.22.clone.1 | convolution fusion | flops 1378876416 | bytes 22602756 | tf_op jit(solution)/shard_map/while/body/eval_jaxpr/dot_general | solution.py:39
  225.7 4.8 %fusion.36 = f32[1024]{0:T(1024)S(1)} fusion(f32[1024,5120]{1,0:T(8,128)S(1)} %get-tuple-element.260, f32[1024]{0:T(1024)S(1)} %get-tuple-element.261), kind=kLoop, calls=%fused_computation.4.clone.1 | loop fusion | flops 10484736 | bytes 20979712 | tf_op jit(solution)/shard_map/while/body/eval_jaxpr/reduce_sum | solution.py:52
  230.5 5.5 %fusion.37 = bf16[5,1024,128]{2,1,0:T(8,128)(2,1)} fusion(bf16[5,1024,128]{2,1,0:T(8,128)(2,1)} %get-tuple-element.298, s32[]{:T(128)} %get-tuple-element.297, bf16[5120,128]{1,0:T(8,128)(2,1)} %get-tuple-element.319, f32[1024,5120]{1,0:T(8,128)S(1)} %get-tuple-element.260, f32[1024]{0:T(1024)S(1)} %get-tuple-element.261, f32[1024]{0:T(1024)S(1)} %fusion.36), kind=kOutput, calls=%fused_computation.11.clone.1 | convolution fusion | flops 1352925184 | bytes 22553088 | tf_op jit(solution)/shard_map/while/body/eval_jaxpr/dot_general | solution.py:53
  236.0 0.6 dynamic_slice.26
  237.2 0.7 dynamic_slice.28
  237.9 8.6 %fusion.35 = (f32[1024]{0:T(1024)S(1)}, f32[1024,5120]{1,0:T(8,128)S(1)}) fusion(bf16[5120,128]{1,0:T(8,128)(2,1)} %get-tuple-element.318, bf16[5120,128]{1,0:T(8,128)(2,1)} %get-tuple-element.317, s32[]{:T(128)S(6)} %select_n.22, s32[1024]{0:T(1024)S(1)} %dynamic_slice.27, s32[5120]{0:T(1024)} %get-tuple-element.315, ...), kind=kOutput, calls=%fused_computation.22.clone.1 | convolution fusion | flops 1378876416 | bytes 22602756 | tf_op jit(solution)/shard_map/while/body/eval_jaxpr/dot_general | solution.py:39
  246.5 4.8 %fusion.36 = f32[1024]{0:T(1024)S(1)} fusion(f32[1024,5120]{1,0:T(8,128)S(1)} %get-tuple-element.260, f32[1024]{0:T(1024)S(1)} %get-tuple-element.261), kind=kLoop, calls=%fused_computation.4.clone.1 | loop fusion | flops 10484736 | bytes 20979712 | tf_op jit(solution)/shard_map/while/body/eval_jaxpr/reduce_sum | solution.py:52
  251.4 5.5 %fusion.37 = bf16[5,1024,128]{2,1,0:T(8,128)(2,1)} fusion(bf16[5,1024,128]{2,1,0:T(8,128)(2,1)} %get-tuple-element.298, s32[]{:T(128)} %get-tuple-element.297, bf16[5120,128]{1,0:T(8,128)(2,1)} %get-tuple-element.319, f32[1024,5120]{1,0:T(8,128)S(1)} %get-tuple-element.260, f32[1024]{0:T(1024)S(1)} %get-tuple-element.261, f32[1024]{0:T(1024)S(1)} %fusion.36), kind=kOutput, calls=%fused_computation.11.clone.1 | convolution fusion | flops 1352925184 | bytes 22553088 | tf_op jit(solution)/shard_map/while/body/eval_jaxpr/dot_general | solution.py:53
  256.8 0.6 dynamic_slice.26
  258.1 0.7 dynamic_slice.28
  258.8 8.6 %fusion.35 = (f32[1024]{0:T(1024)S(1)}, f32[1024,5120]{1,0:T(8,128)S(1)}) fusion(bf16[5120,128]{1,0:T(8,128)(2,1)} %get-tuple-element.318, bf16[5120,128]{1,0:T(8,128)(2,1)} %get-tuple-element.317, s32[]{:T(128)S(6)} %select_n.22, s32[1024]{0:T(1024)S(1)} %dynamic_slice.27, s32[5120]{0:T(1024)} %get-tuple-element.315, ...), kind=kOutput, calls=%fused_computation.22.clone.1 | convolution fusion | flops 1378876416 | bytes 22602756 | tf_op jit(solution)/shard_map/while/body/eval_jaxpr/dot_general | solution.py:39
  267.4 4.8 %fusion.36 = f32[1024]{0:T(1024)S(1)} fusion(f32[1024,5120]{1,0:T(8,128)S(1)} %get-tuple-element.260, f32[1024]{0:T(1024)S(1)} %get-tuple-element.261), kind=kLoop, calls=%fused_computation.4.clone.1 | loop fusion | flops 10484736 | bytes 20979712 | tf_op jit(solution)/shard_map/while/body/eval_jaxpr/reduce_sum | solution.py:52
  272.3 5.5 %fusion.37 = bf16[5,1024,128]{2,1,0:T(8,128)(2,1)} fusion(bf16[5,1024,128]{2,1,0:T(8,128)(2,1)} %get-tuple-element.298, s32[]{:T(128)} %get-tuple-element.297, bf16[5120,128]{1,0:T(8,128)(2,1)} %get-tuple-element.319, f32[1024,5120]{1,0:T(8,128)S(1)} %get-tuple-element.260, f32[1024]{0:T(1024)S(1)} %get-tuple-element.261, f32[1024]{0:T(1024)S(1)} %fusion.36), kind=kOutput, calls=%fused_computation.11.clone.1 | convolution fusion | flops 1352925184 | bytes 22553088 | tf_op jit(solution)/shard_map/while/body/eval_jaxpr/dot_general | solution.py:53
  277.7 3.2 %reshape.66 = bf16[320,2048]{1,0:T(8,128)(2,1)} reshape(bf16[5,1024,128]{2,1,0:T(8,128)(2,1)} %get-tuple-element.122) | data formatting | bytes 2621440 | tf_op jit(solution)/shard_map/reshape | solution.py:57
  (56 shorter events, 1.9 us)
Async XLA Ops:
  4.5 10.9 %collective-permute-start = (bf16[2,320,128]{2,1,0:T(8,128)(2,1)S(1)}, bf16[2,320,128]{2,1,0:T(8,128)(2,1)S(1)}, u32[]{:S(2)}, u32[]{:S(2)}) collective-permute-start(bf16[2,320,128]{2,1,0:T(8,128)(2,1)S(1)} %get-tuple-element.270), channel_id=1, source_target_pairs={{0,1},{1,2},{2,3},{3,4},{4,5},{5,6},{6,7},{7,8},{8,9},{9,10},{10,1... | collective-permute-start | bytes 491528 | tf_op jit(solution)/shard_map/while/body/eval_jaxpr/ppermute | solution.py:12
  15.4 10.9 %collective-permute-start = (bf16[2,320,128]{2,1,0:T(8,128)(2,1)S(1)}, bf16[2,320,128]{2,1,0:T(8,128)(2,1)S(1)}, u32[]{:S(2)}, u32[]{:S(2)}) collective-permute-start(bf16[2,320,128]{2,1,0:T(8,128)(2,1)S(1)} %get-tuple-element.270), channel_id=1, source_target_pairs={{0,1},{1,2},{2,3},{3,4},{4,5},{5,6},{6,7},{7,8},{8,9},{9,10},{10,1... | collective-permute-start | bytes 491528 | tf_op jit(solution)/shard_map/while/body/eval_jaxpr/ppermute | solution.py:12
  26.3 10.9 %collective-permute-start = (bf16[2,320,128]{2,1,0:T(8,128)(2,1)S(1)}, bf16[2,320,128]{2,1,0:T(8,128)(2,1)S(1)}, u32[]{:S(2)}, u32[]{:S(2)}) collective-permute-start(bf16[2,320,128]{2,1,0:T(8,128)(2,1)S(1)} %get-tuple-element.270), channel_id=1, source_target_pairs={{0,1},{1,2},{2,3},{3,4},{4,5},{5,6},{6,7},{7,8},{8,9},{9,10},{10,1... | collective-permute-start | bytes 491528 | tf_op jit(solution)/shard_map/while/body/eval_jaxpr/ppermute | solution.py:12
  37.2 10.9 %collective-permute-start = (bf16[2,320,128]{2,1,0:T(8,128)(2,1)S(1)}, bf16[2,320,128]{2,1,0:T(8,128)(2,1)S(1)}, u32[]{:S(2)}, u32[]{:S(2)}) collective-permute-start(bf16[2,320,128]{2,1,0:T(8,128)(2,1)S(1)} %get-tuple-element.270), channel_id=1, source_target_pairs={{0,1},{1,2},{2,3},{3,4},{4,5},{5,6},{6,7},{7,8},{8,9},{9,10},{10,1... | collective-permute-start | bytes 491528 | tf_op jit(solution)/shard_map/while/body/eval_jaxpr/ppermute | solution.py:12
  48.2 10.9 %collective-permute-start = (bf16[2,320,128]{2,1,0:T(8,128)(2,1)S(1)}, bf16[2,320,128]{2,1,0:T(8,128)(2,1)S(1)}, u32[]{:S(2)}, u32[]{:S(2)}) collective-permute-start(bf16[2,320,128]{2,1,0:T(8,128)(2,1)S(1)} %get-tuple-element.270), channel_id=1, source_target_pairs={{0,1},{1,2},{2,3},{3,4},{4,5},{5,6},{6,7},{7,8},{8,9},{9,10},{10,1... | collective-permute-start | bytes 491528 | tf_op jit(solution)/shard_map/while/body/eval_jaxpr/ppermute | solution.py:12
  59.1 10.9 %collective-permute-start = (bf16[2,320,128]{2,1,0:T(8,128)(2,1)S(1)}, bf16[2,320,128]{2,1,0:T(8,128)(2,1)S(1)}, u32[]{:S(2)}, u32[]{:S(2)}) collective-permute-start(bf16[2,320,128]{2,1,0:T(8,128)(2,1)S(1)} %get-tuple-element.270), channel_id=1, source_target_pairs={{0,1},{1,2},{2,3},{3,4},{4,5},{5,6},{6,7},{7,8},{8,9},{9,10},{10,1... | collective-permute-start | bytes 491528 | tf_op jit(solution)/shard_map/while/body/eval_jaxpr/ppermute | solution.py:12
  70.0 10.9 %collective-permute-start = (bf16[2,320,128]{2,1,0:T(8,128)(2,1)S(1)}, bf16[2,320,128]{2,1,0:T(8,128)(2,1)S(1)}, u32[]{:S(2)}, u32[]{:S(2)}) collective-permute-start(bf16[2,320,128]{2,1,0:T(8,128)(2,1)S(1)} %get-tuple-element.270), channel_id=1, source_target_pairs={{0,1},{1,2},{2,3},{3,4},{4,5},{5,6},{6,7},{7,8},{8,9},{9,10},{10,1... | collective-permute-start | bytes 491528 | tf_op jit(solution)/shard_map/while/body/eval_jaxpr/ppermute | solution.py:12
  80.9 10.9 %collective-permute-start = (bf16[2,320,128]{2,1,0:T(8,128)(2,1)S(1)}, bf16[2,320,128]{2,1,0:T(8,128)(2,1)S(1)}, u32[]{:S(2)}, u32[]{:S(2)}) collective-permute-start(bf16[2,320,128]{2,1,0:T(8,128)(2,1)S(1)} %get-tuple-element.270), channel_id=1, source_target_pairs={{0,1},{1,2},{2,3},{3,4},{4,5},{5,6},{6,7},{7,8},{8,9},{9,10},{10,1... | collective-permute-start | bytes 491528 | tf_op jit(solution)/shard_map/while/body/eval_jaxpr/ppermute | solution.py:12
  91.8 10.9 %collective-permute-start = (bf16[2,320,128]{2,1,0:T(8,128)(2,1)S(1)}, bf16[2,320,128]{2,1,0:T(8,128)(2,1)S(1)}, u32[]{:S(2)}, u32[]{:S(2)}) collective-permute-start(bf16[2,320,128]{2,1,0:T(8,128)(2,1)S(1)} %get-tuple-element.270), channel_id=1, source_target_pairs={{0,1},{1,2},{2,3},{3,4},{4,5},{5,6},{6,7},{7,8},{8,9},{9,10},{10,1... | collective-permute-start | bytes 491528 | tf_op jit(solution)/shard_map/while/body/eval_jaxpr/ppermute | solution.py:12
  102.8 10.9 %collective-permute-start = (bf16[2,320,128]{2,1,0:T(8,128)(2,1)S(1)}, bf16[2,320,128]{2,1,0:T(8,128)(2,1)S(1)}, u32[]{:S(2)}, u32[]{:S(2)}) collective-permute-start(bf16[2,320,128]{2,1,0:T(8,128)(2,1)S(1)} %get-tuple-element.270), channel_id=1, source_target_pairs={{0,1},{1,2},{2,3},{3,4},{4,5},{5,6},{6,7},{7,8},{8,9},{9,10},{10,1... | collective-permute-start | bytes 491528 | tf_op jit(solution)/shard_map/while/body/eval_jaxpr/ppermute | solution.py:12
  113.7 10.9 %collective-permute-start = (bf16[2,320,128]{2,1,0:T(8,128)(2,1)S(1)}, bf16[2,320,128]{2,1,0:T(8,128)(2,1)S(1)}, u32[]{:S(2)}, u32[]{:S(2)}) collective-permute-start(bf16[2,320,128]{2,1,0:T(8,128)(2,1)S(1)} %get-tuple-element.270), channel_id=1, source_target_pairs={{0,1},{1,2},{2,3},{3,4},{4,5},{5,6},{6,7},{7,8},{8,9},{9,10},{10,1... | collective-permute-start | bytes 491528 | tf_op jit(solution)/shard_map/while/body/eval_jaxpr/ppermute | solution.py:12
  124.6 10.9 %collective-permute-start = (bf16[2,320,128]{2,1,0:T(8,128)(2,1)S(1)}, bf16[2,320,128]{2,1,0:T(8,128)(2,1)S(1)}, u32[]{:S(2)}, u32[]{:S(2)}) collective-permute-start(bf16[2,320,128]{2,1,0:T(8,128)(2,1)S(1)} %get-tuple-element.270), channel_id=1, source_target_pairs={{0,1},{1,2},{2,3},{3,4},{4,5},{5,6},{6,7},{7,8},{8,9},{9,10},{10,1... | collective-permute-start | bytes 491528 | tf_op jit(solution)/shard_map/while/body/eval_jaxpr/ppermute | solution.py:12
  135.5 10.9 %collective-permute-start = (bf16[2,320,128]{2,1,0:T(8,128)(2,1)S(1)}, bf16[2,320,128]{2,1,0:T(8,128)(2,1)S(1)}, u32[]{:S(2)}, u32[]{:S(2)}) collective-permute-start(bf16[2,320,128]{2,1,0:T(8,128)(2,1)S(1)} %get-tuple-element.270), channel_id=1, source_target_pairs={{0,1},{1,2},{2,3},{3,4},{4,5},{5,6},{6,7},{7,8},{8,9},{9,10},{10,1... | collective-permute-start | bytes 491528 | tf_op jit(solution)/shard_map/while/body/eval_jaxpr/ppermute | solution.py:12
  146.4 10.9 %collective-permute-start = (bf16[2,320,128]{2,1,0:T(8,128)(2,1)S(1)}, bf16[2,320,128]{2,1,0:T(8,128)(2,1)S(1)}, u32[]{:S(2)}, u32[]{:S(2)}) collective-permute-start(bf16[2,320,128]{2,1,0:T(8,128)(2,1)S(1)} %get-tuple-element.270), channel_id=1, source_target_pairs={{0,1},{1,2},{2,3},{3,4},{4,5},{5,6},{6,7},{7,8},{8,9},{9,10},{10,1... | collective-permute-start | bytes 491528 | tf_op jit(solution)/shard_map/while/body/eval_jaxpr/ppermute | solution.py:12
  157.4 10.9 %collective-permute-start = (bf16[2,320,128]{2,1,0:T(8,128)(2,1)S(1)}, bf16[2,320,128]{2,1,0:T(8,128)(2,1)S(1)}, u32[]{:S(2)}, u32[]{:S(2)}) collective-permute-start(bf16[2,320,128]{2,1,0:T(8,128)(2,1)S(1)} %get-tuple-element.270), channel_id=1, source_target_pairs={{0,1},{1,2},{2,3},{3,4},{4,5},{5,6},{6,7},{7,8},{8,9},{9,10},{10,1... | collective-permute-start | bytes 491528 | tf_op jit(solution)/shard_map/while/body/eval_jaxpr/ppermute | solution.py:12
where the time goes:
time: 282 us; the launch traced here: 281 us
  waiting for transfers between devices  134 us (48%)
  matrix products  70.4 us (25%)
  starting transfers between devices  28.8 us (10%)
  other arithmetic  26.3 us (9%)
  local copies, waits for them, and re-layouts  17.8 us (6%)
  loops' own time  3.81 us (1%)
    ppermute x15, waiting for transfers between devices, from_behind(): return lax.ppermute(block, axis, route)  134 us
    dot_general x5, matrix products, one_block(): lax.dot_general(piece, keys, (((1,), (1,)), ((), ())), preferred_element_...  43 us
    ppermute x15, starting transfers between devices, from_behind(): return lax.ppermute(block, axis, route)  28.8 us
    dot_general x5, matrix products, one_block(): jnp.dot(probs.astype(jnp.bfloat16), values, preferred_element_type=jnp.fl...  27.3 us
    reduce_sum x5, other arithmetic, one_block(): total = jnp.sum(probs, axis=1)  24.1 us
  transfers between devices with their start and end apart: 15, of which 15 were waited for; matrix products, arithmetic and copies ran while one was open for 0% of the time, Pallas kernels for 0%

commit v1 on v0

v1 whole, which is shorter than its diff:
```python
import functools

import jax
import jax.numpy as jnp
from jax import lax
from jax.experimental import pallas as pl
from jax.experimental.pallas import tpu as pltpu
from jax.sharding import PartitionSpec as P

AXES = ("outer", "inner")
ROW = 8
TOK = 320
HD = 128
HEADS = 16
GROUP = 4
M = GROUP * TOK
NDOCS = 64
SCALE = 1.4426950408889634 / HD**0.5
F32 = jnp.float32
BF16 = jnp.bfloat16


def permute(block, source_of):
    return lax.ppermute(block, AXES, [(source_of(i), i) for i in range(128)])


def doc_starts(doc_ref, first, last):
    def step(i, carry):
        end, a, b = carry
        end = end + doc_ref[i]
        return end, jnp.where(end <= first, end, a), jnp.where(end <= last, end, b)

    zero = jnp.int32(0)
    _, a, b = lax.fori_loop(0, NDOCS, step, (zero, zero, zero))
    return a, b


def stack_heads(q_ref):
    return jnp.concatenate([q_ref[:, i * HD : (i + 1) * HD] for i in range(GROUP)], 0)


def scores_t(k, q):
    return lax.dot_general(k, q, (((1,), (1,)), ((), ())), preferred_element_type=F32)


def weigh(v, p):
    return lax.dot_general(
        v, p.astype(BF16), (((0,), (0,)), ((), ())), preferred_element_type=F32
    )


def fold(p):
    return functools.reduce(lambda a, b: a + b, [p[i : i + 8] for i in range(0, p.shape[0], 8)])


def own_kernel(info, docs, q_ref, kv_ref, acc_ref, tot_ref, m_ref, start_ref):
    token = lax.broadcasted_iota(jnp.int32, (1, TOK), 1)

    @pl.when(pl.program_id(0) == 0)
    def _():
        base = info[0] * TOK

        def step(i, carry):
            end, begin = carry
            end = end + docs[i]
            return end, jnp.where(end <= token, end, begin)

        low = jnp.full((1, TOK), -(1 << 20), jnp.int32)
        _, begin = lax.fori_loop(0, NDOCS, step, (-base, jnp.maximum(low, -base)))
        start_ref[...] = jnp.concatenate([begin] * GROUP, 1)

    q = stack_heads(q_ref)
    s = scores_t(kv_ref[:TOK], q) * SCALE
    key = lax.broadcasted_iota(jnp.int32, (TOK, M), 0)
    row = jnp.concatenate([token] * GROUP, 1)
    s = jnp.where((key <= row) & (key >= start_ref[...]), s, F32(-1e30))
    m = jnp.max(s, 0, keepdims=True)
    p = jnp.exp2(s - m)
    m_ref[...] = m
    tot_ref[...] = fold(p)
    acc_ref[...] = weigh(kv_ref[TOK:], p)


def add_blocks(q, blocks, m, start, masked):
    k = jnp.concatenate([b[0] for b in blocks], 0)
    v = jnp.concatenate([b[1] for b in blocks], 0)
    p = jnp.exp2(scores_t(k, q) * SCALE - m)
    if masked:
        key = lax.broadcasted_iota(jnp.int32, (TOK, M), 0)
        keep = [key >= start - b[2] for b in blocks]
        p = jnp.where(jnp.concatenate(keep, 0), p, F32(0))
    return weigh(v, p), fold(p)


def span(ref, *at):
    return ref[(*at, slice(0, TOK))], ref[(*at, slice(TOK, 2 * TOK))]


def three_blocks(core, z_ref, zo_ref):
    side = (1 - 2 * core) * TOK
    return [
        (*span(z_ref), -8 * TOK),
        (*span(zo_ref, 0), -8 * TOK + side),
        (*span(zo_ref, 1), jnp.where(core == 0, -15 * TOK, -TOK)),
    ]


def four_blocks(core, shift, wrap, x_ref, xo_ref):
    side = (1 - 2 * core) * TOK
    near = -2 * shift * TOK
    far = near - 8 * TOK
    at = 1 - wrap
    return [
        (*span(x_ref, at), near),
        (*span(xo_ref, at), near + side),
        (*span(x_ref, wrap), far),
        (*span(xo_ref, wrap), far + side),
    ]


def chunk(q, blocks, state, m, start, first, last, near=None):
    acc_in, tot_in, acc_out, tot_out = state
    lowest = functools.reduce(jnp.minimum, [b[2] for b in blocks])
    highest = functools.reduce(jnp.maximum, [b[2] for b in blocks]) + TOK - 1
    full = last <= lowest
    if near is None:
        some = first <= highest
    else:
        some = first <= functools.reduce(jnp.maximum, [b[2] for b in blocks[near:]]) + TOK - 1

    def put(part, masked):
        acc, tot = add_blocks(q, part, m, start, masked)
        acc_out[...] = acc_in[...] + acc
        tot_out[...] = tot_in[...] + tot

    @pl.when(full)
    def _():
        put(blocks, False)

    @pl.when(jnp.logical_not(full) & some)
    def _():
        put(blocks, True)

    rest = jnp.logical_not(full) & jnp.logical_not(some)
    if near is not None:
        few = rest & (first <= highest)
        rest = rest & (first > highest)

        @pl.when(few)
        def _():
            put(blocks[:near], True)

    @pl.when(rest)
    def _():
        acc_out[...] = acc_in[...]
        tot_out[...] = tot_in[...]


def bounds(info, docs):
    base = info[0] * TOK
    first, last = doc_starts(docs, base, base + TOK - 1)
    return first - base, last - base


def z_kernel(info, docs, q_ref, z_ref, zo_ref, m_ref, start_ref, acc_in, tot_in, acc, tot):
    first, last = bounds(info, docs)
    blocks = three_blocks(info[1], z_ref, zo_ref)
    state = (acc_in, tot_in, acc, tot)
    chunk(stack_heads(q_ref), blocks, state, m_ref[...], start_ref[...], first, last)


def x_kernel(shift, info, docs, q_ref, x_ref, xo_ref, m_ref, start_ref, acc_in, tot_in, acc, tot):
    first, last = bounds(info, docs)
    blocks = four_blocks(info[1], shift, info[1 + shift], x_ref, xo_ref)
    state = (acc_in, tot_in, acc, tot)
    chunk(stack_heads(q_ref), blocks, state, m_ref[...], start_ref[...], first, last, near=2)


def last_kernel(
    shift, info, docs, q_ref, x_ref, xo_ref, m_ref, start_ref, acc_in, tot_in, *rest
):
    sources, (out_ref, acc, tot, window, sem) = rest[:-5], rest[-5:]
    first, last = bounds(info, docs)
    q = stack_heads(q_ref)
    core = info[1]
    blocks = four_blocks(core, shift, info[1 + shift], x_ref, xo_ref)
    state = (acc_in, tot_in, acc, tot)
    chunk(q, blocks, state, m_ref[...], start_ref[...], first, last, near=2)

    total = jnp.sum(tot[...], 0, keepdims=True)

    def put(result):
        for i in range(GROUP):
            part = result[:, i * TOK : (i + 1) * TOK].T
            out_ref[:, i * HD : (i + 1) * HD] = part.astype(BF16)

    put(acc[...] / total)

    @pl.when(jnp.logical_not(jnp.max(total) < F32(1e30)))
    def _():
        kv, z, zo, xs, xos = sources
        side = jnp.where(core == 0, 1, -1)
        pieces = [(kv, 0), (z, -8), (zo.at[0], side - 8), (zo.at[1], jnp.where(core == 0, -15, -1))]
        for s, x, xo in zip((1, 3, 2), xs, xos):
            wrap = info[1 + s]
            for half in (0, 1):
                far = jnp.where(wrap == half, -8, 0)
                pieces += [(x.at[half], far - 2 * s), (xo.at[half], far - 2 * s + side)]
        for piece, place in pieces:
            copy = pltpu.make_async_copy(piece, window.at[place + 15], sem)
            copy.start()
            copy.wait()

        row = jnp.concatenate([lax.broadcasted_iota(jnp.int32, (1, TOK), 1)] * GROUP, 1)

        def step(i, carry):
            top, acc_c, tot_c = carry
            block = 15 - i
            s = scores_t(window[block, :TOK], q) * SCALE
            key = lax.broadcasted_iota(jnp.int32, (TOK, M), 0) + (block - 15) * TOK
            keep = (key <= row) & (key >= start_ref[...])
            s = jnp.where(keep, s, F32(-1e30))
            new = jnp.maximum(top, jnp.max(s, 0, keepdims=True))
            p = jnp.where(keep, jnp.exp2(s - new), F32(0))
            decay = jnp.exp2(top - new)
            return new, acc_c * decay + weigh(window[block, TOK:], p), tot_c * decay + fold(p)

        zero = (jnp.full((1, M), -1e30, F32), jnp.zeros((HD, M), F32), jnp.zeros((8, M), F32))
        _, acc_c, tot_c = lax.fori_loop(0, 16, step, zero)
        put(acc_c / jnp.sum(tot_c, 0, keepdims=True))


def flat(kernel):
    def wrapped(info, docs, q, x, xo, m, start, acc_in, tot_in, *rest):
        refs = list(rest)
        sources = [refs[0], refs[1], refs[2], refs[3:6], refs[6:9]]
        return kernel(info, docs, q, x, xo, m, start, acc_in, tot_in, *sources, *refs[9:])

    return wrapped


SMEM = pl.BlockSpec(memory_space=pltpu.SMEM)
Q_SPEC = pl.BlockSpec((TOK, GROUP * HD), lambda g: (0, g))
ACC_SPEC = pl.BlockSpec((HD, M), lambda g: (0, g))
TOT_SPEC = pl.BlockSpec((8, M), lambda g: (0, g))
M_SPEC = pl.BlockSpec((1, M), lambda g: (0, g))
START_SPEC = pl.BlockSpec((1, M), lambda g: (0, 0))
ANY = pl.BlockSpec(memory_space=pl.ANY)
ACC = jax.ShapeDtypeStruct((HD, HEADS * TOK), F32)
TOT = jax.ShapeDtypeStruct((8, HEADS * TOK), F32)


def whole(array):
    return pl.BlockSpec(array.shape, lambda g: (0,) * array.ndim)


def cost(keys):
    rows = HEADS * TOK
    return pl.CostEstimate(
        flops=4 * rows * keys * HD, bytes_accessed=8 * 2**20, transcendentals=rows * keys
    )


PARAMS = pltpu.CompilerParams(
    vmem_limit_bytes=56 * 2**20, dimension_semantics=("arbitrary",)
)


def shards(queries, keys, values, doc_lengths):
    device = lax.axis_index(AXES)
    core = device % 2
    col = device % ROW // 2
    info = jnp.stack([device, core] + [(col < s).astype(jnp.int32) for s in (1, 2, 3)])
    info = info.astype(jnp.int32)
    own = jnp.concatenate([keys, values], 0)

    z1 = permute(own, lambda i: (i - ROW) % 128)
    z2 = permute(own, lambda i: (i - 2 * ROW) % 128)

    grid = (HEADS // GROUP,)
    acc, tot, m, start = pl.pallas_call(
        own_kernel,
        grid=grid,
        out_shape=(
            ACC,
            TOT,
            jax.ShapeDtypeStruct((1, HEADS * TOK), F32),
            jax.ShapeDtypeStruct((1, M), jnp.int32),
        ),
        in_specs=[SMEM, SMEM, Q_SPEC, whole(own)],
        out_specs=(ACC_SPEC, TOT_SPEC, M_SPEC, START_SPEC),
        compiler_params=PARAMS,
        cost_estimate=cost(TOK),
        name="own",
    )(info, doc_lengths, queries, own)

    z_other = permute(jnp.stack([z1, jnp.where(core == 0, own, z2)]), lambda i: i ^ 1)
    xs, xos = [], []
    for s in (1, 3, 2):
        message = jnp.stack([z1, jnp.where(col + s < 4, own, z2)])
        got = permute(message, lambda i: i // ROW * ROW + (i % ROW - 2 * s) % ROW)
        xs.append(got)
    for got in xs:
        xos.append(permute(got, lambda i: i ^ 1))

    acc, tot = pl.pallas_call(
        z_kernel,
        grid=grid,
        out_shape=(ACC, TOT),
        in_specs=[SMEM, SMEM, Q_SPEC, whole(z1), whole(z_other), M_SPEC, START_SPEC, ACC_SPEC, TOT_SPEC],
        out_specs=(ACC_SPEC, TOT_SPEC),
        input_output_aliases={7: 0, 8: 1},
        compiler_params=PARAMS,
        cost_estimate=cost(3 * TOK),
        name="zpart",
    )(info, doc_lengths, queries, z1, z_other, m, start, acc, tot)

    for s, x, xo in list(zip((1, 3, 2), xs, xos))[:2]:
        acc, tot = pl.pallas_call(
            functools.partial(x_kernel, s),
            grid=grid,
            out_shape=(ACC, TOT),
            in_specs=[SMEM, SMEM, Q_SPEC, whole(x), whole(xo), M_SPEC, START_SPEC, ACC_SPEC, TOT_SPEC],
            out_specs=(ACC_SPEC, TOT_SPEC),
            input_output_aliases={7: 0, 8: 1},
            compiler_params=PARAMS,
            cost_estimate=cost(4 * TOK),
            name="xpart",
        )(info, doc_lengths, queries, x, xo, m, start, acc, tot)

    x, xo = xs[2], xos[2]
    return pl.pallas_call(
        flat(functools.partial(last_kernel, 2)),
        grid=grid,
        out_shape=jax.ShapeDtypeStruct(queries.shape, BF16),
        in_specs=[SMEM, SMEM, Q_SPEC, whole(x), whole(xo), M_SPEC, START_SPEC, ACC_SPEC, TOT_SPEC]
        + [ANY] * 9,
        out_specs=Q_SPEC,
        scratch_shapes=[
            pltpu.VMEM((HD, M), F32),
            pltpu.VMEM((8, M), F32),
            pltpu.VMEM((16, 2 * TOK, HD), BF16),
            pltpu.SemaphoreType.DMA,
        ],
        compiler_params=PARAMS,
        cost_estimate=cost(4 * TOK),
        name="lastpart",
    )(info, doc_lengths, queries, x, xo, m, start, acc, tot, own, z1, z_other, *xs, *xos)


def solution(mesh):
    rows = P(AXES, None)
    return jax.shard_map(
        shards, mesh=mesh, in_specs=(rows, rows, rows, P()), out_specs=rows, check_vma=False
    )
```

time: 282 us -> 92 us (0.33)
  the two profiles are of different devices: /device:TPU:16 before, /device:TPU:26 now
where the time goes in v1:
time: 92 us; the launch traced here: 92.1 us
  Pallas kernels  62 us (67%)
  waiting for transfers between devices  14.5 us (16%)
  starting transfers between devices  9.82 us (11%)
  local copies, waits for them, and re-layouts  5.4 us (6%)
    pallas_call x2, Pallas kernels, shards(): pl.pallas_call(functools.partial(x_kernel, s), grid=grid, out_shape=(ACC,...  28.4 us
    pallas_call x1, Pallas kernels, shards(): pl.pallas_call(flat(functools.partial(last_kernel, 2)), grid=grid, out_sh...  15.1 us
    ppermute x9, waiting for transfers between devices, permute(): return lax.ppermute(block, AXES, [(source_of(i), i) for i in range(128)])  14.5 us
    pallas_call x1, Pallas kernels, shards(): pl.pallas_call(z_kernel, grid=grid, out_shape=(ACC, TOT), in_specs=[SMEM,...  11.7 us
    ppermute x9, starting transfers between devices, permute(): return lax.ppermute(block, AXES, [(source_of(i), i) for i in range(128)])  9.82 us
    pallas_call x1, Pallas kernels, shards(): pl.pallas_call(own_kernel, grid=grid, out_shape=(ACC, TOT, jax.ShapeDtype...  6.88 us
    unnamed x19, local copies, waits for them, and re-layouts  3.82 us
  transfers between devices with their start and end apart: 9, of which 3 were waited for; matrix products, arithmetic and copies ran while one was open for 1% of the time, Pallas kernels for 51%

profile of v1, /device:TPU:26, one launch (start us, length us, event | category | flops | bytes accessed | tf_op | source)
XLA Modules:
  0.0 92.1 jit_solution(13069126852927091328)
XLA Ops:
  0.0 0.9 constant_dynamic-update-slice_fusion.1
  0.9 0.9 constant_dynamic-update-slice_fusion.kv_ref.rest_0_
  1.8 0.0 copy-start
  1.8 3.9 %collective-permute-start.1 = (bf16[640,128]{1,0:T(8,128)(2,1)S(1)}, bf16[640,128]{1,0:T(8,128)(2,1)S(1)}, u32[]{:S(2)}, u32[]{:S(2)}) collective-permute-start(bf16[640,128]{1,0:T(8,128)(2,1)S(1)} %constant_dynamic-update-slice_fusion.kv_ref.rest_0_), channel_id=1, source_target_pairs={{112,0},{113,1},{114,2},{115,3},{116,4},{117,5},{118,6},{119,7},{1... | collective-permute-start | bytes 491528 | tf_op jit(solution)/shard_map/ppermute | solution.py:24
  5.7 1.0 %collective-permute-start = (bf16[640,128]{1,0:T(8,128)(2,1)S(1)}, bf16[640,128]{1,0:T(8,128)(2,1)S(1)}, u32[]{:S(2)}, u32[]{:S(2)}) collective-permute-start(bf16[640,128]{1,0:T(8,128)(2,1)S(1)} %constant_dynamic-update-slice_fusion.kv_ref.rest_0_), channel_id=1, source_target_pairs={{120,0},{121,1},{122,2},{123,3},{124,4},{125,5},{126,6},{127,7},{0... | collective-permute-start | bytes 491528 | tf_op jit(solution)/shard_map/ppermute | solution.py:24
  6.8 3.6 %collective-permute-done.1 = bf16[640,128]{1,0:T(8,128)(2,1)S(1)} collective-permute-done((bf16[640,128]{1,0:T(8,128)(2,1)S(1)}, bf16[640,128]{1,0:T(8,128)(2,1)S(1)}, u32[]{:S(2)}, u32[]{:S(2)}) %collective-permute-start.1) | collective-permute-done | bytes 163872 | tf_op jit(solution)/shard_map/ppermute | solution.py:24
  10.4 4.3 %collective-permute-done.z_ref.rest_1_ = bf16[640,128]{1,0:T(8,128)(2,1)S(1)} collective-permute-done((bf16[640,128]{1,0:T(8,128)(2,1)S(1)}, bf16[640,128]{1,0:T(8,128)(2,1)S(1)}, u32[]{:S(2)}, u32[]{:S(2)}) %collective-permute-start) | collective-permute-done | bytes 163872 | tf_op jit(solution)/shard_map/ppermute | solution.py:24
  14.8 0.0 copy-start.1
  14.8 0.1 pad_maximum_fusion
  14.9 1.6 %collective-permute-start.6 = (bf16[2,640,128]{2,1,0:T(8,128)(2,1)S(1)}, bf16[2,640,128]{2,1,0:T(8,128)(2,1)S(1)}, u32[]{:S(2)}, u32[]{:S(2)}) collective-permute-start(bf16[2,640,128]{2,1,0:T(8,128)(2,1)S(1)} %get-tuple-element.31), channel_id=1, source_target_pairs={{6,0},{7,1},{0,2},{1,3},{2,4},{3,5},{4,6},{5,7},{14,8},{15,9},{8,1... | collective-permute-start | bytes 983048 | tf_op jit(solution)/shard_map/ppermute | solution.py:24
  16.4 0.5 collective-permute-start.4
  17.0 2.1 %collective-permute-start.2 = (bf16[2,640,128]{2,1,0:T(8,128)(2,1)S(1)}, bf16[2,640,128]{2,1,0:T(8,128)(2,1)S(1)}, u32[]{:S(2)}, u32[]{:S(2)}) collective-permute-start(bf16[2,640,128]{2,1,0:T(8,128)(2,1)S(1)} %get-tuple-element.32), channel_id=1, source_target_pairs={{4,0},{5,1},{6,2},{7,3},{0,4},{1,5},{2,6},{3,7},{12,8},{13,9},{14,... | collective-permute-start | bytes 983048 | tf_op jit(solution)/shard_map/ppermute | solution.py:24
  19.1 0.0 collective-permute-start.8
  19.1 6.5 %collective-permute-done.6.x_ref.rest_3_ = bf16[2,640,128]{2,1,0:T(8,128)(2,1)S(1)} collective-permute-done((bf16[2,640,128]{2,1,0:T(8,128)(2,1)S(1)}, bf16[2,640,128]{2,1,0:T(8,128)(2,1)S(1)}, u32[]{:S(2)}, u32[]{:S(2)}) %collective-permute-start.6) | collective-permute-done | bytes 327712 | tf_op jit(solution)/shard_map/ppermute | solution.py:24
  25.6 0.0 copy-start.2
  25.6 0.0 collective-permute-start.7
  25.6 0.7 stack.65.info
  26.3 0.0 copy-done
  26.3 6.9 %own.1 = (f32[128,5120]{1,0:T(8,128)}, f32[8,5120]{1,0:T(8,128)}, f32[1,5120]{1,0:T(1,128)}, s32[1,1280]{1,0:T(1,128)}) custom-call(s32[5]{0:T(128)} %stack.65.info, s32[64]{0:T(128)} %docs.9, bf16[320,2048]{1,0:T(8,128)(2,1)} %q.1, bf16[640,128]{1,0:T(8,128)(2,1)} %copy-done), custom_call_target="tpu_custom_call" | custom-call | flops 838860800 | bytes 8388608 | tf_op jit(solution)/shard_map/own/pallas_call | solution.py:281
  33.2 0.0 copy-done.1
  33.2 0.0 collective-permute-done.4.x_ref.rest_4_
  33.2 0.0 copy-start.3
  33.2 0.5 collective-permute-start.5
  33.7 0.0 collective-permute-done.2.x.rest_5_
  33.7 0.0 copy-start.4
  33.7 0.1 collective-permute-start.3
  33.8 0.0 collective-permute-done.8.zo_ref.rest_2_
  33.8 0.0 copy-start.5
  33.8 0.7 copy-done.5
  34.6 11.7 %zpart.1 = (f32[128,5120]{1,0:T(8,128)}, f32[8,5120]{1,0:T(8,128)}) custom-call(s32[5]{0:T(128)} %stack.65.info, s32[64]{0:T(128)} %docs.9, bf16[320,2048]{1,0:T(8,128)(2,1)} %q.1, bf16[640,128]{1,0:T(8,128)(2,1)} %copy-done.1, bf16[2,640,128]{2,1,0:T(8,128)(2,1)} %copy-done.5, ...), custom_call_target="tpu_custom_call", output_to_operand_aliasing={{0}: (7, {}), {1}: (8, {})} | custom-call | flops 2516582400 | bytes 8388608 | tf_op jit(solution)/shard_map/zpart/pallas_call | solution.py:306
  46.3 0.0 copy-done.2
  46.3 0.0 copy-done.3
  46.3 0.0 copy-done.4
  46.3 0.0 collective-permute-done.7.xo_ref.rest_6_
  46.3 0.0 copy-start.6
  46.3 0.7 copy-done.6
  47.0 14.2 %xpart.2 = (f32[128,5120]{1,0:T(8,128)}, f32[8,5120]{1,0:T(8,128)}) custom-call(s32[5]{0:T(128)} %stack.65.info, s32[64]{0:T(128)} %docs.9, bf16[320,2048]{1,0:T(8,128)(2,1)} %q.1, bf16[2,640,128]{2,1,0:T(8,128)(2,1)} %copy-done.2, bf16[2,640,128]{2,1,0:T(8,128)(2,1)} %copy-done.6, ...), custom_call_target="tpu_custom_call", output_to_operand_aliasing={{0}: (7, {}), {1}: (8, {})} | custom-call | flops 3355443200 | bytes 8388608 | tf_op jit(solution)/shard_map/xpart/pallas_call | solution.py:319
  61.2 0.0 collective-permute-done.5.xo_ref.rest_7_
  61.2 0.0 copy-start.7
  61.2 0.7 copy-done.7
  62.0 14.2 %xpart.3 = (f32[128,5120]{1,0:T(8,128)}, f32[8,5120]{1,0:T(8,128)}) custom-call(s32[5]{0:T(128)} %stack.65.info, s32[64]{0:T(128)} %docs.9, bf16[320,2048]{1,0:T(8,128)(2,1)} %q.1, bf16[2,640,128]{2,1,0:T(8,128)(2,1)} %copy-done.3, bf16[2,640,128]{2,1,0:T(8,128)(2,1)} %copy-done.7, ...), custom_call_target="tpu_custom_call", output_to_operand_aliasing={{0}: (7, {}), {1}: (8, {})} | custom-call | flops 3355443200 | bytes 8388608 | tf_op jit(solution)/shard_map/xpart/pallas_call | solution.py:319
  76.1 0.0 collective-permute-done.3.xo.rest_8_
  76.1 0.0 copy-start.8
  76.2 0.7 copy-done.8
  76.9 15.1 %lastpart.1 = bf16[320,2048]{1,0:T(8,128)(2,1)} custom-call(s32[5]{0:T(128)} %stack.65.info, s32[64]{0:T(128)} %docs.9, bf16[320,2048]{1,0:T(8,128)(2,1)} %q.1, bf16[2,640,128]{2,1,0:T(8,128)(2,1)} %copy-done.4, bf16[2,640,128]{2,1,0:T(8,128)(2,1)} %copy-done.8, f32[1,5120]{1,0:T(1,128)} %get-tuple-element.15.m_ref.m, ...), custom_call_target="tpu_custom_call" | custom-call | flops 3355443200 | bytes 8388608 | tf_op jit(solution)/shard_map/lastpart/pallas_call | solution.py:332
  (1 shorter events, 0.0 us)
Async XLA Ops:
  1.8 24.5 %copy-start = (bf16[640,128]{1,0:T(8,128)(2,1)}, bf16[640,128]{1,0:T(8,128)(2,1)S(1)}, u32[]{:S(2)}) copy-start(bf16[640,128]{1,0:T(8,128)(2,1)S(1)} %constant_dynamic-update-slice_fusion.kv_ref.rest_0_) | copy-start | bytes 491524
  1.8 8.6 %collective-permute-start.1 = (bf16[640,128]{1,0:T(8,128)(2,1)S(1)}, bf16[640,128]{1,0:T(8,128)(2,1)S(1)}, u32[]{:S(2)}, u32[]{:S(2)}) collective-permute-start(bf16[640,128]{1,0:T(8,128)(2,1)S(1)} %constant_dynamic-update-slice_fusion.kv_ref.rest_0_), channel_id=1, source_target_pairs={{112,0},{113,1},{114,2},{115,3},{116,4},{117,5},{118,6},{119,7},{1... | collective-permute-start | bytes 491528 | tf_op jit(solution)/shard_map/ppermute | solution.py:24
  5.7 9.0 %collective-permute-start = (bf16[640,128]{1,0:T(8,128)(2,1)S(1)}, bf16[640,128]{1,0:T(8,128)(2,1)S(1)}, u32[]{:S(2)}, u32[]{:S(2)}) collective-permute-start(bf16[640,128]{1,0:T(8,128)(2,1)S(1)} %constant_dynamic-update-slice_fusion.kv_ref.rest_0_), channel_id=1, source_target_pairs={{120,0},{121,1},{122,2},{123,3},{124,4},{125,5},{126,6},{127,7},{0... | collective-permute-start | bytes 491528 | tf_op jit(solution)/shard_map/ppermute | solution.py:24
  14.8 18.4 %copy-start.1 = (bf16[640,128]{1,0:T(8,128)(2,1)}, bf16[640,128]{1,0:T(8,128)(2,1)S(1)}, u32[]{:S(2)}) copy-start(bf16[640,128]{1,0:T(8,128)(2,1)S(1)} %collective-permute-done.z_ref.rest_1_) | copy-start | bytes 491524
  14.9 10.7 %collective-permute-start.6 = (bf16[2,640,128]{2,1,0:T(8,128)(2,1)S(1)}, bf16[2,640,128]{2,1,0:T(8,128)(2,1)S(1)}, u32[]{:S(2)}, u32[]{:S(2)}) collective-permute-start(bf16[2,640,128]{2,1,0:T(8,128)(2,1)S(1)} %get-tuple-element.31), channel_id=1, source_target_pairs={{6,0},{7,1},{0,2},{1,3},{2,4},{3,5},{4,6},{5,7},{14,8},{15,9},{8,1... | collective-permute-start | bytes 983048 | tf_op jit(solution)/shard_map/ppermute | solution.py:24
  16.4 16.7 %collective-permute-start.4 = (bf16[2,640,128]{2,1,0:T(8,128)(2,1)S(1)}, bf16[2,640,128]{2,1,0:T(8,128)(2,1)S(1)}, u32[]{:S(2)}, u32[]{:S(2)}) collective-permute-start(bf16[2,640,128]{2,1,0:T(8,128)(2,1)S(1)} %get-tuple-element.30), channel_id=1, source_target_pairs={{2,0},{3,1},{4,2},{5,3},{6,4},{7,5},{0,6},{1,7},{10,8},{11,9},{12,... | collective-permute-start | bytes 983048 | tf_op jit(solution)/shard_map/ppermute | solution.py:24
  17.0 16.8 %collective-permute-start.2 = (bf16[2,640,128]{2,1,0:T(8,128)(2,1)S(1)}, bf16[2,640,128]{2,1,0:T(8,128)(2,1)S(1)}, u32[]{:S(2)}, u32[]{:S(2)}) collective-permute-start(bf16[2,640,128]{2,1,0:T(8,128)(2,1)S(1)} %get-tuple-element.32), channel_id=1, source_target_pairs={{4,0},{5,1},{6,2},{7,3},{0,4},{1,5},{2,6},{3,7},{12,8},{13,9},{14,... | collective-permute-start | bytes 983048 | tf_op jit(solution)/shard_map/ppermute | solution.py:24
  19.1 14.7 %collective-permute-start.8 = (bf16[2,640,128]{2,1,0:T(8,128)(2,1)S(1)}, bf16[2,640,128]{2,1,0:T(8,128)(2,1)S(1)}, u32[]{:S(2)}, u32[]{:S(2)}) collective-permute-start(bf16[2,640,128]{2,1,0:T(8,128)(2,1)S(1)} %get-tuple-element.29), channel_id=1, source_target_pairs={{1,0},{0,1},{3,2},{2,3},{5,4},{4,5},{7,6},{6,7},{9,8},{8,9},{11,10... | collective-permute-start | bytes 983048 | tf_op jit(solution)/shard_map/ppermute | solution.py:24
  25.6 20.7 %copy-start.2 = (bf16[2,640,128]{2,1,0:T(8,128)(2,1)}, bf16[2,640,128]{2,1,0:T(8,128)(2,1)S(1)}, u32[]{:S(2)}) copy-start(bf16[2,640,128]{2,1,0:T(8,128)(2,1)S(1)} %collective-permute-done.6.x_ref.rest_3_) | copy-start | bytes 983044
  25.6 20.7 %collective-permute-start.7 = (bf16[2,640,128]{2,1,0:T(8,128)(2,1)S(1)}, bf16[2,640,128]{2,1,0:T(8,128)(2,1)S(1)}, u32[]{:S(2)}, u32[]{:S(2)}) collective-permute-start(bf16[2,640,128]{2,1,0:T(8,128)(2,1)S(1)} %collective-permute-done.6.x_ref.rest_3_), channel_id=1, source_target_pairs={{1,0},{0,1},{3,2},{2,3},{5,4},{4,5},{7,6},{6,7},{9,8},{8,9},{11,10... | collective-permute-start | bytes 983048 | tf_op jit(solution)/shard_map/ppermute | solution.py:24
  33.2 13.1 %copy-start.3 = (bf16[2,640,128]{2,1,0:T(8,128)(2,1)}, bf16[2,640,128]{2,1,0:T(8,128)(2,1)S(1)}, u32[]{:S(2)}) copy-start(bf16[2,640,128]{2,1,0:T(8,128)(2,1)S(1)} %collective-permute-done.4.x_ref.rest_4_) | copy-start | bytes 983044
  33.2 28.0 %collective-permute-start.5 = (bf16[2,640,128]{2,1,0:T(8,128)(2,1)S(1)}, bf16[2,640,128]{2,1,0:T(8,128)(2,1)S(1)}, u32[]{:S(2)}, u32[]{:S(2)}) collective-permute-start(bf16[2,640,128]{2,1,0:T(8,128)(2,1)S(1)} %collective-permute-done.4.x_ref.rest_4_), channel_id=1, source_target_pairs={{1,0},{0,1},{3,2},{2,3},{5,4},{4,5},{7,6},{6,7},{9,8},{8,9},{11,10... | collective-permute-start | bytes 983048 | tf_op jit(solution)/shard_map/ppermute | solution.py:24
  33.7 12.6 %copy-start.4 = (bf16[2,640,128]{2,1,0:T(8,128)(2,1)}, bf16[2,640,128]{2,1,0:T(8,128)(2,1)S(1)}, u32[]{:S(2)}) copy-start(bf16[2,640,128]{2,1,0:T(8,128)(2,1)S(1)} %collective-permute-done.2.x.rest_5_) | copy-start | bytes 983044
  33.7 42.4 %collective-permute-start.3 = (bf16[2,640,128]{2,1,0:T(8,128)(2,1)S(1)}, bf16[2,640,128]{2,1,0:T(8,128)(2,1)S(1)}, u32[]{:S(2)}, u32[]{:S(2)}) collective-permute-start(bf16[2,640,128]{2,1,0:T(8,128)(2,1)S(1)} %collective-permute-done.2.x.rest_5_), channel_id=1, source_target_pairs={{1,0},{0,1},{3,2},{2,3},{5,4},{4,5},{7,6},{6,7},{9,8},{8,9},{11,10... | collective-permute-start | bytes 983048 | tf_op jit(solution)/shard_map/ppermute | solution.py:24
  33.8 0.7 copy-start.5
  46.3 0.7 copy-start.6
  61.2 0.7 copy-start.7
  76.1 0.7 copy-start.8

commit v2 on v0

v2 whole, which is shorter than its diff:
```python
import functools

import jax
import jax.numpy as jnp
from jax import lax
from jax.experimental import pallas as pl
from jax.experimental.pallas import tpu as pltpu
from jax.sharding import PartitionSpec as P

AXES = ("outer", "inner")
ROW = 8
TOK = 320
HD = 128
HEADS = 16
GROUP = 4
GROUPS = HEADS // GROUP
M = GROUP * TOK
NDOCS = 64
DEVICES = 128
SCALE = 1.4426950408889634 / HD**0.5
NEVER = -1e30
F32 = jnp.float32
BF16 = jnp.bfloat16
MIB = 2**20


def place():
    device = lax.axis_index("outer") * 64 + lax.axis_index("inner")
    return device, lax.rem(device, 2)


def columns(g, width=M):
    return pl.ds(pl.multiple_of(g * width, width), width)


def dot(a, b):
    return jnp.dot(a, b, preferred_element_type=F32)


def fold(p):
    return functools.reduce(lambda a, b: a + b, [p[i : i + 8] for i in range(0, p.shape[0], 8)])


def causal(begin):
    key = lax.broadcasted_iota(jnp.int32, (TOK, TOK), 0)
    row = lax.broadcasted_iota(jnp.int32, (TOK, TOK), 1)
    return jnp.where((key <= row) & (key >= begin), F32(0), F32(NEVER))


def own_kernel(docs, q_ref, kv_ref, qt_ref, acc_ref, tot_ref, begin_ref, first_ref, bias_ref):
    device, _ = place()
    token = lax.broadcasted_iota(jnp.int32, (1, TOK), 1)
    end = -device * TOK
    first = end
    begin = jnp.full((1, TOK), end, jnp.int32)
    for i in range(NDOCS):
        end = end + docs[i]
        begin = jnp.where(end <= token, end, begin)
        first = jnp.where(end <= 0, end, first)
    first_ref[0] = first
    begin_ref[...] = jnp.concatenate([begin] * GROUP, 1)
    bias_ref[...] = jnp.concatenate([causal(begin)] * GROUP, 1)
    qt_ref[HD:, :] = jnp.zeros((HD, HEADS * TOK), BF16)
    k = kv_ref[:TOK]
    vt = kv_ref[TOK:].T

    @pl.loop(0, GROUPS)
    def _(g):
        heads = [q_ref[:, columns(g * GROUP + i, HD)] for i in range(GROUP)]
        qt = jnp.concatenate(heads, 0).T
        qt_ref[:HD, columns(g)] = qt
        s = dot(k, qt) + bias_ref[...]
        m = jnp.max(s, 0, keepdims=True).astype(BF16).astype(F32)
        p = jnp.exp2((s - m) * SCALE)
        tot_ref[:, columns(g)] = fold(p)
        acc_ref[:, columns(g)] = dot(vt, p.astype(BF16))
        shift = jnp.where(begin_ref[...] < 0, -m, F32(NEVER))
        line = lax.broadcasted_iota(jnp.int32, (16, M), 0)
        extra = jnp.where(line == 0, shift, jnp.where(line == 1, F32(1), F32(0)))
        qt_ref[HD : HD + 16, columns(g)] = extra.astype(BF16)


def fill(blocks, first, k_ref, vt_ref):
    for i, (block, position) in enumerate(blocks):
        rows = slice(i * TOK, (i + 1) * TOK)
        k_ref[rows, :HD] = block[:TOK]
        key = lax.broadcasted_iota(jnp.int32, (TOK, HD), 0) + position
        lane = lax.broadcasted_iota(jnp.int32, (TOK, HD), 1)
        late = jnp.where(key >= first, F32(0), F32(NEVER))
        bias = jnp.where(lane == 0, F32(1), jnp.where(lane == 1, late, F32(0)))
        k_ref[rows, HD:] = bias.astype(BF16)
    vt_ref[...] = jnp.concatenate([block[TOK:] for block, _ in blocks], 0).T


def pair(ours, theirs, step, side):
    return [(ours, step * TOK), (theirs, (step + side) * TOK)]


def partial(g, qt_ref, k_ref, vt_ref):
    p = jnp.exp2(dot(k_ref[...], qt_ref[:, columns(g)]) * SCALE)
    return dot(vt_ref[...], p.astype(BF16)), fold(p)


def middle_kernel(steps, first_ref, qt_ref, ours, theirs, acc_in, tot_in, acc, tot, k_ref, vt_ref):
    _, core = place()
    side = 1 - 2 * core
    first = first_ref[0]

    @pl.when(first < (max(steps) + 2) * TOK)
    def _():
        blocks = []
        for i, step in enumerate(steps):
            at = pl.ds(i * 2 * TOK, 2 * TOK)
            blocks += pair(ours.at[at], theirs.at[at], step, side)
        fill(blocks, first, k_ref, vt_ref)

        @pl.loop(0, GROUPS)
        def _(g):
            a, t = partial(g, qt_ref, k_ref, vt_ref)
            acc[:, columns(g)] = acc_in[:, columns(g)] + a
            tot[:, columns(g)] = tot_in[:, columns(g)] + t


def last_kernel(
    first_ref, qt_ref, x_ref, far, far2, near, near2, z, z2, own, begin_ref, acc, tot,
    out_hbm, k_ref, vt_ref, out_ref, window, sems,
):
    _, core = place()
    side = 1 - 2 * core
    first = first_ref[0]
    x_step = jnp.where(core == 0, -15, -1)
    blocks = [(x_ref, x_step * TOK)]
    for i, step in enumerate((-10, -12, -14)):
        at = pl.ds(i * 2 * TOK, 2 * TOK)
        blocks += pair(far.at[at], far2.at[at], step, side)
    some = first < jnp.where(core == 0, -8, 0) * TOK

    @pl.when(some)
    def _():
        fill(blocks, first, k_ref, vt_ref)

    def send(g):
        return pltpu.make_async_copy(
            out_ref.at[lax.rem(g, 2)], out_hbm.at[:, columns(g, GROUP * HD)], sems.at[lax.rem(g, 2)]
        )

    def put(g, result):
        for i in range(GROUP):
            part = result[:, i * TOK : (i + 1) * TOK].T
            out_ref[lax.rem(g, 2), :, i * HD : (i + 1) * HD] = part.astype(BF16)

    @pl.loop(0, GROUPS)
    def _(g):
        @pl.when(g >= 2)
        def _():
            send(g - 2).wait()

        def finish(a, t):
            total = jnp.sum(t, 0, keepdims=True)
            put(g, a / total)
            return jnp.max(total)

        def with_blocks():
            a, t = partial(g, qt_ref, k_ref, vt_ref)
            return finish(acc[:, columns(g)] + a, tot[:, columns(g)] + t)

        def without():
            return finish(acc[:, columns(g)], tot[:, columns(g)])

        largest = lax.cond(some, with_blocks, without)

        @pl.when(jnp.logical_not(largest < F32(1e30)))
        def _():
            pieces = [(own, 0), (x_ref, x_step), (z, -8), (z2, side - 8)]
            for i in range(3):
                at = pl.ds(i * 2 * TOK, 2 * TOK)
                pieces += [(near.at[at], -2 - 2 * i), (near2.at[at], side - 2 - 2 * i)]
                pieces += [(far.at[at], -10 - 2 * i), (far2.at[at], side - 10 - 2 * i)]
            for piece, step in pieces:
                window[step + 15] = piece[...]
            q = qt_ref[:HD, columns(g)]
            row = jnp.concatenate([lax.broadcasted_iota(jnp.int32, (1, TOK), 1)] * GROUP, 1)

            def step(i, carry):
                top, a, t = carry
                s = dot(window[15 - i, :TOK], q) * SCALE
                key = lax.broadcasted_iota(jnp.int32, (TOK, M), 0) - i * TOK
                keep = (key <= row) & (key >= begin_ref[...])
                s = jnp.where(keep, s, F32(NEVER))
                new = jnp.maximum(top, jnp.max(s, 0, keepdims=True))
                p = jnp.where(keep, jnp.exp2(s - new), F32(0))
                decay = jnp.exp2(top - new)
                return new, a * decay + dot(window[15 - i, TOK:].T, p.astype(BF16)), t * decay + fold(p)

            zero = (jnp.full((1, M), NEVER, F32), jnp.zeros((HD, M), F32), jnp.zeros((8, M), F32))
            _, a, t = lax.fori_loop(0, 16, step, zero)
            put(g, a / jnp.sum(t, 0, keepdims=True))

        send(g).start()

    for g in (GROUPS - 2, GROUPS - 1):
        send(g).wait()


VMEM = pl.BlockSpec(memory_space=pltpu.VMEM)
SMEM = pl.BlockSpec(memory_space=pltpu.SMEM)
QT = pltpu.VMEM((2 * HD, HEADS * TOK), BF16)
ACC = pltpu.VMEM((HD, HEADS * TOK), F32)
TOT = pltpu.VMEM((8, HEADS * TOK), F32)


def params(mib):
    return pltpu.CompilerParams(vmem_limit_bytes=mib * MIB)


def cost(keys):
    rows = HEADS * TOK
    return pl.CostEstimate(
        flops=8 * rows * keys * HD, bytes_accessed=MIB, transcendentals=rows * keys
    )


def layout(keys):
    return [pltpu.VMEM((keys, 2 * HD), BF16), pltpu.VMEM((HD, keys), BF16)]


def chip(array):
    return pltpu.with_memory_space_constraint(array, pltpu.VMEM)


def permute(block, pairs):
    return lax.ppermute(block, AXES, pairs)


def shift_row(block):
    return permute(block, [(i, i + ROW) for i in range(DEVICES - ROW)])


def swap(block):
    return permute(block, [(i, i ^ 1) for i in range(DEVICES)])


def own_part(queries, own, doc_lengths):
    return pl.pallas_call(
        own_kernel,
        out_shape=(
            QT, ACC, TOT, pltpu.VMEM((1, M), jnp.int32), jax.ShapeDtypeStruct((1,), jnp.int32)
        ),
        in_specs=[SMEM, VMEM, VMEM],
        out_specs=(VMEM, VMEM, VMEM, VMEM, SMEM),
        scratch_shapes=[pltpu.VMEM((TOK, M), F32)],
        compiler_params=params(16),
        cost_estimate=cost(TOK),
        name="own",
    )(doc_lengths, chip(queries), chip(own))


def middle_part(steps, first, qt, ours, theirs, acc, tot):
    keys = 2 * TOK * len(steps)
    return pl.pallas_call(
        functools.partial(middle_kernel, steps),
        out_shape=(ACC, TOT),
        in_specs=[SMEM] + [VMEM] * 5,
        out_specs=(VMEM, VMEM),
        scratch_shapes=layout(keys),
        input_output_aliases={4: 0, 5: 1},
        compiler_params=params(28),
        cost_estimate=cost(keys),
        name="middle",
    )(first, *[chip(x) for x in (qt, ours, theirs, acc, tot)])


def last_part(first, arrays, shape):
    return pl.pallas_call(
        last_kernel,
        out_shape=jax.ShapeDtypeStruct(shape, BF16),
        in_specs=[SMEM] + [VMEM] * len(arrays),
        out_specs=pl.BlockSpec(memory_space=pl.ANY),
        scratch_shapes=layout(7 * TOK)
        + [
            pltpu.VMEM((2, TOK, GROUP * HD), BF16),
            pltpu.VMEM((16, 2 * TOK, HD), BF16),
            pltpu.SemaphoreType.DMA((2,)),
        ],
        compiler_params=params(36),
        cost_estimate=cost(7 * TOK),
        name="last",
    )(first, *[chip(x) for x in arrays])


def shards(queries, keys, values, doc_lengths):
    col = lax.axis_index("inner") % ROW // 2
    own = jnp.concatenate([keys, values], 0)

    z = shift_row(own)
    x = permute(own, [(i, i + 1) for i in range(0, DEVICES, 2)]
                + [(i, i + 15) for i in range(1, DEVICES - 15, 2)])
    qt, acc, tot, begin, first = own_part(queries, own, doc_lengths)
    z, acc, tot = lax.optimization_barrier((z, acc, tot))

    near = []
    for s in (1, 2, 3):
        message = jnp.where(col + s < ROW // 2, own, z)
        route = [(i, i // ROW * ROW + (i + 2 * s) % ROW) for i in range(DEVICES)]
        near.append(permute(message, route))
    z2 = swap(z)
    acc, tot = middle_part((-8,), first, qt, z, z2, acc, tot)

    near = jnp.concatenate(near, 0)
    far = shift_row(near)
    near2 = swap(near)
    acc, tot = middle_part((-2, -4, -6), first, qt, near, near2, acc, tot)
    far2 = swap(far)
    arrays = (qt, x, far, far2, near, near2, z, z2, own, begin, acc, tot)
    return last_part(first, arrays, queries.shape)


def solution(mesh):
    rows = P(AXES, None)
    return jax.shard_map(
        shards, mesh=mesh, in_specs=(rows, rows, rows, P()), out_specs=rows, check_vma=False
    )
```

time: 282 us -> 68.6 us (0.24)
  the two profiles are of different devices: /device:TPU:16 before, /device:TPU:27 now
where the time goes in v2:
time: 68.6 us; the launch traced here: 68.3 us
  Pallas kernels  29.2 us (43%)
  starting transfers between devices  20.3 us (30%)
  waiting for transfers between devices  14.7 us (21%)
  local copies, waits for them, and re-layouts  3.81 us (6%)
    ppermute x9, starting transfers between devices, permute(): return lax.ppermute(block, AXES, pairs)  20.3 us
    ppermute x9, waiting for transfers between devices, permute(): return lax.ppermute(block, AXES, pairs)  14.7 us
    pallas_call x1, Pallas kernels, last_part(): pl.pallas_call(last_kernel, out_shape=jax.ShapeDtypeStruct(shape, BF16),...  14 us
    pallas_call x2, Pallas kernels, middle_part(): pl.pallas_call(functools.partial(middle_kernel, steps), out_shape=(ACC, T...  10.7 us
    pallas_call x1, Pallas kernels, own_part(): pl.pallas_call(own_kernel, out_shape=(QT, ACC, TOT, pltpu.VMEM((1, M), jn...  4.52 us
    unnamed x7, local copies, waits for them, and re-layouts  2.89 us
  transfers between devices with their start and end apart: 9, of which 4 were waited for; matrix products, arithmetic and copies ran while one was open for 0% of the time, Pallas kernels for 22%

profile of v2, /device:TPU:27, one launch (start us, length us, event | category | flops | bytes accessed | tf_op | source)
XLA Modules:
  0.0 68.3 jit_solution(9123607781365500467)
XLA Ops:
  0.0 0.9 %constant_dynamic-update-slice_fusion.1 = bf16[640,128]{1,0:T(8,128)(2,1)S(1)} fusion(bf16[320,128]{1,0:T(8,128)(2,1)} %param.5), kind=kLoop, calls=%fused_computation.4 | loop fusion | bytes 163840
  0.9 0.9 %constant_dynamic-update-slice_fusion.kv_ref.own = bf16[640,128]{1,0:T(8,128)(2,1)S(1)} fusion(bf16[640,128]{1,0:T(8,128)(2,1)S(1)} %constant_dynamic-update-slice_fusion.1, bf16[320,128]{1,0:T(8,128)(2,1)} %param.6), kind=kLoop, calls=%fused_computation.3 | loop fusion | bytes 163840 | tf_op jit(solution)/shard_map/concatenate | solution.py:293
  1.8 3.5 %collective-permute-start.1 = (bf16[640,128]{1,0:T(8,128)(2,1)S(1)}, bf16[640,128]{1,0:T(8,128)(2,1)S(1)}, u32[]{:S(2)}, u32[]{:S(2)}) collective-permute-start(bf16[640,128]{1,0:T(8,128)(2,1)S(1)} %constant_dynamic-update-slice_fusion.kv_ref.own), channel_id=1, source_target_pairs={{0,8},{1,9},{2,10},{3,11},{4,12},{5,13},{6,14},{7,15},{8,16},{9,17... | collective-permute-start | bytes 491528 | tf_op jit(solution)/shard_map/ppermute | solution.py:232
  5.4 0.0 copy-start
  5.4 1.3 %copy-done = bf16[320,2048]{1,0:T(8,128)(2,1)S(1)} copy-done((bf16[320,2048]{1,0:T(8,128)(2,1)S(1)}, bf16[320,2048]{1,0:T(8,128)(2,1)}, u32[]{:S(2)}) %copy-start) | copy-done | bytes 1310744
  6.7 0.0 copy-start.1
  6.7 0.7 copy-done.1
  7.4 4.5 %own.1 = (bf16[256,5120]{1,0:T(8,128)(2,1)S(1)}, f32[128,5120]{1,0:T(8,128)S(1)}, f32[8,5120]{1,0:T(8,128)S(1)}, s32[1,1280]{1,0:T(1,128)S(1)}, s32[1]{0:T(128)}) custom-call(s32[64]{0:T(128)S(1)} %copy-done.1, bf16[320,2048]{1,0:T(8,128)(2,1)S(1)} %copy-done, bf16[640,128]{1,0:T(8,128)(2,1)S(1)} %constant_dynamic-update-slice_fusion.kv_ref.own), custom_call_target="tpu_custom_call" | custom-call | flops 1677721600 | bytes 1048576 | tf_op jit(solution)/shard_map/own/pallas_call | solution.py:244
  11.9 0.0 collective-permute-done.1.ours.z
  12.0 1.3 %collective-permute-start.2 = (bf16[640,128]{1,0:T(8,128)(2,1)S(1)}, bf16[640,128]{1,0:T(8,128)(2,1)S(1)}, u32[]{:S(2)}, u32[]{:S(2)}) collective-permute-start(bf16[640,128]{1,0:T(8,128)(2,1)S(1)} %get-tuple-element.31), channel_id=1, source_target_pairs={{0,2},{1,3},{2,4},{3,5},{4,6},{5,7},{6,0},{7,1},{8,10},{9,11},{10,... | collective-permute-start | bytes 491528 | tf_op jit(solution)/shard_map/ppermute | solution.py:232
  13.2 0.8 %collective-permute-start.3 = (bf16[640,128]{1,0:T(8,128)(2,1)S(1)}, bf16[640,128]{1,0:T(8,128)(2,1)S(1)}, u32[]{:S(2)}, u32[]{:S(2)}) collective-permute-start(bf16[640,128]{1,0:T(8,128)(2,1)S(1)} %get-tuple-element.30), channel_id=1, source_target_pairs={{0,4},{1,5},{2,6},{3,7},{4,0},{5,1},{6,2},{7,3},{8,12},{9,13},{10,... | collective-permute-start | bytes 491528 | tf_op jit(solution)/shard_map/ppermute | solution.py:232
  14.1 1.9 %collective-permute-start.4 = (bf16[640,128]{1,0:T(8,128)(2,1)S(1)}, bf16[640,128]{1,0:T(8,128)(2,1)S(1)}, u32[]{:S(2)}, u32[]{:S(2)}) collective-permute-start(bf16[640,128]{1,0:T(8,128)(2,1)S(1)} %get-tuple-element.29), channel_id=1, source_target_pairs={{0,6},{1,7},{2,0},{3,1},{4,2},{5,3},{6,4},{7,5},{8,14},{9,15},{10,... | collective-permute-start | bytes 491528 | tf_op jit(solution)/shard_map/ppermute | solution.py:232
  15.9 0.8 %collective-permute-done.2 = bf16[640,128]{1,0:T(8,128)(2,1)S(1)} collective-permute-done((bf16[640,128]{1,0:T(8,128)(2,1)S(1)}, bf16[640,128]{1,0:T(8,128)(2,1)S(1)}, u32[]{:S(2)}, u32[]{:S(2)}) %collective-permute-start.2) | collective-permute-done | bytes 163872 | tf_op jit(solution)/shard_map/ppermute | solution.py:232
  16.8 2.5 %collective-permute-done.3 = bf16[640,128]{1,0:T(8,128)(2,1)S(1)} collective-permute-done((bf16[640,128]{1,0:T(8,128)(2,1)S(1)}, bf16[640,128]{1,0:T(8,128)(2,1)S(1)}, u32[]{:S(2)}, u32[]{:S(2)}) %collective-permute-start.3) | collective-permute-done | bytes 163872 | tf_op jit(solution)/shard_map/ppermute | solution.py:232
  19.3 3.6 %collective-permute-done.4 = bf16[640,128]{1,0:T(8,128)(2,1)S(1)} collective-permute-done((bf16[640,128]{1,0:T(8,128)(2,1)S(1)}, bf16[640,128]{1,0:T(8,128)(2,1)S(1)}, u32[]{:S(2)}, u32[]{:S(2)}) %collective-permute-start.4) | collective-permute-done | bytes 163872 | tf_op jit(solution)/shard_map/ppermute | solution.py:232
  23.0 3.6 %collective-permute-start.5 = (bf16[1920,128]{1,0:T(8,128)(2,1)S(1)}, bf16[1920,128]{1,0:T(8,128)(2,1)S(1)}, u32[]{:S(2)}, u32[]{:S(2)}) collective-permute-start(bf16[1920,128]{1,0:T(8,128)(2,1)S(1)} %constant_dynamic-update-slice_fusion.2.ours.near), channel_id=1, source_target_pairs={{0,8},{1,9},{2,10},{3,11},{4,12},{5,13},{6,14},{7,15},{8,16},{9,17... | collective-permute-start | bytes 1474568 | tf_op jit(solution)/shard_map/ppermute | solution.py:232
  26.5 1.6 %collective-permute-start.7 = (bf16[1920,128]{1,0:T(8,128)(2,1)S(1)}, bf16[1920,128]{1,0:T(8,128)(2,1)S(1)}, u32[]{:S(2)}, u32[]{:S(2)}) collective-permute-start(bf16[1920,128]{1,0:T(8,128)(2,1)S(1)} %constant_dynamic-update-slice_fusion.2.ours.near), channel_id=1, source_target_pairs={{0,1},{1,0},{2,3},{3,2},{4,5},{5,4},{6,7},{7,6},{8,9},{9,8},{10,11... | collective-permute-start | bytes 1474568 | tf_op jit(solution)/shard_map/ppermute | solution.py:232
  28.1 0.1 collective-permute-start.8
  28.2 3.6 %collective-permute-start = (bf16[640,128]{1,0:T(8,128)(2,1)S(1)}, bf16[640,128]{1,0:T(8,128)(2,1)S(1)}, u32[]{:S(2)}, u32[]{:S(2)}) collective-permute-start(bf16[640,128]{1,0:T(8,128)(2,1)S(1)} %constant_dynamic-update-slice_fusion.kv_ref.own), channel_id=1, source_target_pairs={{0,1},{2,3},{4,5},{6,7},{8,9},{10,11},{12,13},{14,15},{16,17},{18,... | collective-permute-start | bytes 491528 | tf_op jit(solution)/shard_map/ppermute | solution.py:232
  31.8 0.0 collective-permute-done.8.theirs.z2
  31.8 0.6 middle.2
  32.5 7.7 %collective-permute-done.5.far = bf16[1920,128]{1,0:T(8,128)(2,1)S(1)} collective-permute-done((bf16[1920,128]{1,0:T(8,128)(2,1)S(1)}, bf16[1920,128]{1,0:T(8,128)(2,1)S(1)}, u32[]{:S(2)}, u32[]{:S(2)}) %collective-permute-start.5) | collective-permute-done | bytes 491552 | tf_op jit(solution)/shard_map/ppermute | solution.py:232
  40.2 3.9 %collective-permute-start.6 = (bf16[1920,128]{1,0:T(8,128)(2,1)S(1)}, bf16[1920,128]{1,0:T(8,128)(2,1)S(1)}, u32[]{:S(2)}, u32[]{:S(2)}) collective-permute-start(bf16[1920,128]{1,0:T(8,128)(2,1)S(1)} %collective-permute-done.5.far), channel_id=1, source_target_pairs={{0,1},{1,0},{2,3},{3,2},{4,5},{5,4},{6,7},{7,6},{8,9},{9,8},{10,11... | collective-permute-start | bytes 1474568 | tf_op jit(solution)/shard_map/ppermute | solution.py:232
  44.1 0.0 collective-permute-done.7.theirs.near2
  44.1 10.0 %middle.3 = (f32[128,5120]{1,0:T(8,128)S(1)}, f32[8,5120]{1,0:T(8,128)S(1)}) custom-call(s32[1]{0:T(128)} %get-tuple-element.17.first_ref, bf16[256,5120]{1,0:T(8,128)(2,1)S(1)} %get-tuple-element.18.qt_ref, bf16[1920,128]{1,0:T(8,128)(2,1)S(1)} %constant_dynamic-update-slice_fusion.2.ours.near, ...), custom_call_target="tpu_custom_call", output_to_operand_aliasing={{0}: (4, {}), {1}: (5, {})} | custom-call | flops 10066329600 | bytes 1048576 | tf_op jit(solution)/shard_map/middle/pallas_call | solution.py:260
  54.1 0.0 collective-permute-done.x_ref
  54.1 0.0 collective-permute-done.6.far2
  54.1 14.0 %last.1 = bf16[320,2048]{1,0:T(8,128)(2,1)} custom-call(s32[1]{0:T(128)} %get-tuple-element.17.first_ref, bf16[256,5120]{1,0:T(8,128)(2,1)S(1)} %get-tuple-element.18.qt_ref, bf16[640,128]{1,0:T(8,128)(2,1)S(1)} %collective-permute-done.x_ref, bf16[1920,128]{1,0:T(8,128)(2,1)S(1)} %collective-permute-done.5.far, ...), custom_call_target="tpu_custom_call" | custom-call | flops 11744051200 | bytes 1048576 | tf_op jit(solution)/shard_map/last/pallas_call | solution.py:274
  (4 shorter events, 0.1 us)
Async XLA Ops:
  1.8 10.1 %collective-permute-start.1 = (bf16[640,128]{1,0:T(8,128)(2,1)S(1)}, bf16[640,128]{1,0:T(8,128)(2,1)S(1)}, u32[]{:S(2)}, u32[]{:S(2)}) collective-permute-start(bf16[640,128]{1,0:T(8,128)(2,1)S(1)} %constant_dynamic-update-slice_fusion.kv_ref.own), channel_id=1, source_target_pairs={{0,8},{1,9},{2,10},{3,11},{4,12},{5,13},{6,14},{7,15},{8,16},{9,17... | collective-permute-start | bytes 491528 | tf_op jit(solution)/shard_map/ppermute | solution.py:232
  5.4 1.3 %copy-start = (bf16[320,2048]{1,0:T(8,128)(2,1)S(1)}, bf16[320,2048]{1,0:T(8,128)(2,1)}, u32[]{:S(2)}) copy-start(bf16[320,2048]{1,0:T(8,128)(2,1)} %q_ref.1) | copy-start | bytes 3932164
  6.7 0.7 copy-start.1
  12.0 4.8 %collective-permute-start.2 = (bf16[640,128]{1,0:T(8,128)(2,1)S(1)}, bf16[640,128]{1,0:T(8,128)(2,1)S(1)}, u32[]{:S(2)}, u32[]{:S(2)}) collective-permute-start(bf16[640,128]{1,0:T(8,128)(2,1)S(1)} %get-tuple-element.31), channel_id=1, source_target_pairs={{0,2},{1,3},{2,4},{3,5},{4,6},{5,7},{6,0},{7,1},{8,10},{9,11},{10,... | collective-permute-start | bytes 491528 | tf_op jit(solution)/shard_map/ppermute | solution.py:232
  13.2 6.1 %collective-permute-start.3 = (bf16[640,128]{1,0:T(8,128)(2,1)S(1)}, bf16[640,128]{1,0:T(8,128)(2,1)S(1)}, u32[]{:S(2)}, u32[]{:S(2)}) collective-permute-start(bf16[640,128]{1,0:T(8,128)(2,1)S(1)} %get-tuple-element.30), channel_id=1, source_target_pairs={{0,4},{1,5},{2,6},{3,7},{4,0},{5,1},{6,2},{7,3},{8,12},{9,13},{10,... | collective-permute-start | bytes 491528 | tf_op jit(solution)/shard_map/ppermute | solution.py:232
  14.1 8.9 %collective-permute-start.4 = (bf16[640,128]{1,0:T(8,128)(2,1)S(1)}, bf16[640,128]{1,0:T(8,128)(2,1)S(1)}, u32[]{:S(2)}, u32[]{:S(2)}) collective-permute-start(bf16[640,128]{1,0:T(8,128)(2,1)S(1)} %get-tuple-element.29), channel_id=1, source_target_pairs={{0,6},{1,7},{2,0},{3,1},{4,2},{5,3},{6,4},{7,5},{8,14},{9,15},{10,... | collective-permute-start | bytes 491528 | tf_op jit(solution)/shard_map/ppermute | solution.py:232
  23.0 17.2 %collective-permute-start.5 = (bf16[1920,128]{1,0:T(8,128)(2,1)S(1)}, bf16[1920,128]{1,0:T(8,128)(2,1)S(1)}, u32[]{:S(2)}, u32[]{:S(2)}) collective-permute-start(bf16[1920,128]{1,0:T(8,128)(2,1)S(1)} %constant_dynamic-update-slice_fusion.2.ours.near), channel_id=1, source_target_pairs={{0,8},{1,9},{2,10},{3,11},{4,12},{5,13},{6,14},{7,15},{8,16},{9,17... | collective-permute-start | bytes 1474568 | tf_op jit(solution)/shard_map/ppermute | solution.py:232
  26.5 17.5 %collective-permute-start.7 = (bf16[1920,128]{1,0:T(8,128)(2,1)S(1)}, bf16[1920,128]{1,0:T(8,128)(2,1)S(1)}, u32[]{:S(2)}, u32[]{:S(2)}) collective-permute-start(bf16[1920,128]{1,0:T(8,128)(2,1)S(1)} %constant_dynamic-update-slice_fusion.2.ours.near), channel_id=1, source_target_pairs={{0,1},{1,0},{2,3},{3,2},{4,5},{5,4},{6,7},{7,6},{8,9},{9,8},{10,11... | collective-permute-start | bytes 1474568 | tf_op jit(solution)/shard_map/ppermute | solution.py:232
  28.1 3.7 %collective-permute-start.8 = (bf16[640,128]{1,0:T(8,128)(2,1)S(1)}, bf16[640,128]{1,0:T(8,128)(2,1)S(1)}, u32[]{:S(2)}, u32[]{:S(2)}) collective-permute-start(bf16[640,128]{1,0:T(8,128)(2,1)S(1)} %collective-permute-done.1.ours.z), channel_id=1, source_target_pairs={{0,1},{1,0},{2,3},{3,2},{4,5},{5,4},{6,7},{7,6},{8,9},{9,8},{10,11... | collective-permute-start | bytes 491528 | tf_op jit(solution)/shard_map/ppermute | solution.py:232
  28.2 25.9 %collective-permute-start = (bf16[640,128]{1,0:T(8,128)(2,1)S(1)}, bf16[640,128]{1,0:T(8,128)(2,1)S(1)}, u32[]{:S(2)}, u32[]{:S(2)}) collective-permute-start(bf16[640,128]{1,0:T(8,128)(2,1)S(1)} %constant_dynamic-update-slice_fusion.kv_ref.own), channel_id=1, source_target_pairs={{0,1},{2,3},{4,5},{6,7},{8,9},{10,11},{12,13},{14,15},{16,17},{18,... | collective-permute-start | bytes 491528 | tf_op jit(solution)/shard_map/ppermute | solution.py:232
  40.2 14.0 %collective-permute-start.6 = (bf16[1920,128]{1,0:T(8,128)(2,1)S(1)}, bf16[1920,128]{1,0:T(8,128)(2,1)S(1)}, u32[]{:S(2)}, u32[]{:S(2)}) collective-permute-start(bf16[1920,128]{1,0:T(8,128)(2,1)S(1)} %collective-permute-done.5.far), channel_id=1, source_target_pairs={{0,1},{1,0},{2,3},{3,2},{4,5},{5,4},{6,7},{7,6},{8,9},{9,8},{10,11... | collective-permute-start | bytes 1474568 | tf_op jit(solution)/shard_map/ppermute | solution.py:232

commit v3 on v2

--- a/solution.py
+++ b/solution.py
@@ -30,7 +30,7 @@
 
 
 def columns(g, width=M):
-    return pl.ds(pl.multiple_of(g * width, width), width)
+    return pl.ds(g * width if isinstance(g, int) else pl.multiple_of(g * width, width), width)
 
 
 def dot(a, b):
@@ -47,7 +47,31 @@
     return jnp.where((key <= row) & (key >= begin), F32(0), F32(NEVER))
 
 
-def own_kernel(docs, q_ref, kv_ref, qt_ref, acc_ref, tot_ref, begin_ref, first_ref, bias_ref):
+def pack_kernel(k_hbm, v_hbm, kv_ref, sems):
+    copies = [
+        pltpu.make_async_copy(half, kv_ref.at[pl.ds(i * TOK, TOK)], sems.at[i])
+        for i, half in enumerate((k_hbm, v_hbm))
+    ]
+    for copy in copies:
+        copy.start()
+    for copy in copies:
+        copy.wait()
+
+
+def own_kernel(
+    docs_hbm, q_hbm, kv_ref, qt_ref, acc_ref, tot_ref, begin_ref, first_ref,
+    bias_ref, q_ref, docs, sems, docs_sem,
+):
+    read_docs = pltpu.make_async_copy(docs_hbm, docs, docs_sem)
+    read_docs.start()
+
+    def read(g):
+        wide = columns(g, GROUP * HD)
+        return pltpu.make_async_copy(q_hbm.at[:, wide], q_ref.at[:, wide], sems.at[g])
+
+    for g in range(GROUPS):
+        read(g).start()
+    read_docs.wait()
     device, _ = place()
     token = lax.broadcasted_iota(jnp.int32, (1, TOK), 1)
     end = -device * TOK
@@ -66,17 +90,22 @@
 
     @pl.loop(0, GROUPS)
     def _(g):
+        read(g).wait()
         heads = [q_ref[:, columns(g * GROUP + i, HD)] for i in range(GROUP)]
         qt = jnp.concatenate(heads, 0).T
         qt_ref[:HD, columns(g)] = qt
         s = dot(k, qt) + bias_ref[...]
-        m = jnp.max(s, 0, keepdims=True).astype(BF16).astype(F32)
+        m = jnp.max(s, 0, keepdims=True)
         p = jnp.exp2((s - m) * SCALE)
         tot_ref[:, columns(g)] = fold(p)
         acc_ref[:, columns(g)] = dot(vt, p.astype(BF16))
         shift = jnp.where(begin_ref[...] < 0, -m, F32(NEVER))
         line = lax.broadcasted_iota(jnp.int32, (16, M), 0)
-        extra = jnp.where(line == 0, shift, jnp.where(line == 1, F32(1), F32(0)))
+        extra = jnp.where(line == 3, F32(1), F32(0))
+        for i in range(3):
+            part = shift.astype(BF16).astype(F32)
+            extra = jnp.where(line == i, part, extra)
+            shift = shift - part
         qt_ref[HD : HD + 16, columns(g)] = extra.astype(BF16)
 
 
@@ -87,7 +116,7 @@
         key = lax.broadcasted_iota(jnp.int32, (TOK, HD), 0) + position
         lane = lax.broadcasted_iota(jnp.int32, (TOK, HD), 1)
         late = jnp.where(key >= first, F32(0), F32(NEVER))
-        bias = jnp.where(lane == 0, F32(1), jnp.where(lane == 1, late, F32(0)))
+        bias = jnp.where(lane < 3, F32(1), jnp.where(lane == 3, late, F32(0)))
         k_ref[rows, HD:] = bias.astype(BF16)
     vt_ref[...] = jnp.concatenate([block[TOK:] for block, _ in blocks], 0).T
 
@@ -101,17 +130,9 @@
     return dot(vt_ref[...], p.astype(BF16)), fold(p)
 
 
-def middle_kernel(steps, first_ref, qt_ref, ours, theirs, acc_in, tot_in, acc, tot, k_ref, vt_ref):
-    _, core = place()
-    side = 1 - 2 * core
-    first = first_ref[0]
-
-    @pl.when(first < (max(steps) + 2) * TOK)
+def add_all(first, top, blocks, qt_ref, acc_in, tot_in, acc, tot, k_ref, vt_ref):
+    @pl.when(first < top)
     def _():
-        blocks = []
-        for i, step in enumerate(steps):
-            at = pl.ds(i * 2 * TOK, 2 * TOK)
-            blocks += pair(ours.at[at], theirs.at[at], step, side)
         fill(blocks, first, k_ref, vt_ref)
 
         @pl.loop(0, GROUPS)
@@ -119,6 +140,22 @@
             a, t = partial(g, qt_ref, k_ref, vt_ref)
             acc[:, columns(g)] = acc_in[:, columns(g)] + a
             tot[:, columns(g)] = tot_in[:, columns(g)] + t
+
+
+def z_kernel(first_ref, qt_ref, z, z2, x_ref, *state):
+    _, core = place()
+    blocks = pair(z, z2, -8, 1 - 2 * core)
+    blocks.append((x_ref, jnp.where(core == 0, -15, -1) * TOK))
+    add_all(first_ref[0], jnp.where(core == 0, -6, 0) * TOK, blocks, qt_ref, *state)
+
+
+def near_kernel(first_ref, qt_ref, near, near2, *state):
+    _, core = place()
+    blocks = []
+    for i, step in enumerate((-2, -4, -6)):
+        at = pl.ds(i * 2 * TOK, 2 * TOK)
+        blocks += pair(near.at[at], near2.at[at], step, 1 - 2 * core)
+    add_all(first_ref[0], 0, blocks, qt_ref, *state)
 
 
 def last_kernel(
@@ -129,11 +166,11 @@
     side = 1 - 2 * core
     first = first_ref[0]
     x_step = jnp.where(core == 0, -15, -1)
-    blocks = [(x_ref, x_step * TOK)]
+    blocks = []
     for i, step in enumerate((-10, -12, -14)):
         at = pl.ds(i * 2 * TOK, 2 * TOK)
         blocks += pair(far.at[at], far2.at[at], step, side)
-    some = first < jnp.where(core == 0, -8, 0) * TOK
+    some = first < -8 * TOK
 
     @pl.when(some)
     def _():
@@ -204,6 +241,7 @@
 
 VMEM = pl.BlockSpec(memory_space=pltpu.VMEM)
 SMEM = pl.BlockSpec(memory_space=pltpu.SMEM)
+ANY = pl.BlockSpec(memory_space=pl.ANY)
 QT = pltpu.VMEM((2 * HD, HEADS * TOK), BF16)
 ACC = pltpu.VMEM((HD, HEADS * TOK), F32)
 TOT = pltpu.VMEM((8, HEADS * TOK), F32)
@@ -228,6 +266,10 @@
     return pltpu.with_memory_space_constraint(array, pltpu.VMEM)
 
 
+def hbm(array):
+    return pltpu.with_memory_space_constraint(array, pltpu.HBM)
+
+
 def permute(block, pairs):
     return lax.ppermute(block, AXES, pairs)
 
@@ -238,6 +280,18 @@
 
 def swap(block):
     return permute(block, [(i, i ^ 1) for i in range(DEVICES)])
+
+
+def pack(keys, values):
+    return pl.pallas_call(
+        pack_kernel,
+        out_shape=pltpu.VMEM((2 * TOK, HD), BF16),
+        in_specs=[ANY, ANY],
+        out_specs=VMEM,
+        scratch_shapes=[pltpu.SemaphoreType.DMA((2,))],
+        compiler_params=params(4),
+        name="pack",
+    )(hbm(keys), hbm(values))
 
 
 def own_part(queries, own, doc_lengths):
@@ -246,28 +300,34 @@
         out_shape=(
             QT, ACC, TOT, pltpu.VMEM((1, M), jnp.int32), jax.ShapeDtypeStruct((1,), jnp.int32)
         ),
-        in_specs=[SMEM, VMEM, VMEM],
+        in_specs=[ANY, ANY, VMEM],
         out_specs=(VMEM, VMEM, VMEM, VMEM, SMEM),
-        scratch_shapes=[pltpu.VMEM((TOK, M), F32)],
+        scratch_shapes=[
+            pltpu.VMEM((TOK, M), F32),
+            pltpu.VMEM(queries.shape, BF16),
+            pltpu.SMEM((NDOCS,), jnp.int32),
+            pltpu.SemaphoreType.DMA((GROUPS,)),
+            pltpu.SemaphoreType.DMA,
+        ],
         compiler_params=params(16),
         cost_estimate=cost(TOK),
         name="own",
-    )(doc_lengths, chip(queries), chip(own))
-
-
-def middle_part(steps, first, qt, ours, theirs, acc, tot):
-    keys = 2 * TOK * len(steps)
+    )(hbm(doc_lengths), hbm(queries), chip(own))
+
+
+def add_part(kernel, name, keys, first, qt, blocks, acc, tot):
+    at = 2 + len(blocks)
     return pl.pallas_call(
-        functools.partial(middle_kernel, steps),
+        kernel,
         out_shape=(ACC, TOT),
-        in_specs=[SMEM] + [VMEM] * 5,
+        in_specs=[SMEM] + [VMEM] * (3 + len(blocks)),
         out_specs=(VMEM, VMEM),
         scratch_shapes=layout(keys),
-        input_output_aliases={4: 0, 5: 1},
+        input_output_aliases={at: 0, at + 1: 1},
         compiler_params=params(28),
         cost_estimate=cost(keys),
-        name="middle",
-    )(first, *[chip(x) for x in (qt, ours, theirs, acc, tot)])
+        name=name,
+    )(first, *[chip(a) for a in (qt, *blocks, acc, tot)])
 
 
 def last_part(first, arrays, shape):
@@ -276,40 +336,41 @@
         out_shape=jax.ShapeDtypeStruct(shape, BF16),
         in_specs=[SMEM] + [VMEM] * len(arrays),
         out_specs=pl.BlockSpec(memory_space=pl.ANY),
-        scratch_shapes=layout(7 * TOK)
+        scratch_shapes=layout(6 * TOK)
         + [
             pltpu.VMEM((2, TOK, GROUP * HD), BF16),
             pltpu.VMEM((16, 2 * TOK, HD), BF16),
             pltpu.SemaphoreType.DMA((2,)),
         ],
         compiler_params=params(36),
-        cost_estimate=cost(7 * TOK),
+        cost_estimate=cost(6 * TOK),
         name="last",
     )(first, *[chip(x) for x in arrays])
 
 
 def shards(queries, keys, values, doc_lengths):
     col = lax.axis_index("inner") % ROW // 2
-    own = jnp.concatenate([keys, values], 0)
+    own = pack(keys, values)
 
     z = shift_row(own)
     x = permute(own, [(i, i + 1) for i in range(0, DEVICES, 2)]
                 + [(i, i + 15) for i in range(1, DEVICES - 15, 2)])
-    qt, acc, tot, begin, first = own_part(queries, own, doc_lengths)
-    z, acc, tot = lax.optimization_barrier((z, acc, tot))
+    own, z = lax.optimization_barrier((own, z))
 
     near = []
-    for s in (1, 2, 3):
+    for s in (1, 3, 2):
         message = jnp.where(col + s < ROW // 2, own, z)
         route = [(i, i // ROW * ROW + (i + 2 * s) % ROW) for i in range(DEVICES)]
         near.append(permute(message, route))
     z2 = swap(z)
-    acc, tot = middle_part((-8,), first, qt, z, z2, acc, tot)
-
-    near = jnp.concatenate(near, 0)
+    qt, acc, tot, begin, first = own_part(queries, own, doc_lengths)
+
+    near = jnp.concatenate([near[0], near[2], near[1]], 0)
+    near, acc, tot = lax.optimization_barrier((near, acc, tot))
     far = shift_row(near)
     near2 = swap(near)
-    acc, tot = middle_part((-2, -4, -6), first, qt, near, near2, acc, tot)
+    acc, tot = add_part(z_kernel, "zpart", 3 * TOK, first, qt, (z, z2, x), acc, tot)
+    acc, tot = add_part(near_kernel, "nearpart", 6 * TOK, first, qt, (near, near2), acc, tot)
     far2 = swap(far)
     arrays = (qt, x, far, far2, near, near2, z, z2, own, begin, acc, tot)
     return last_part(first, arrays, queries.shape)

time: 68.6 us -> 64.2 us (0.936)
  the two profiles are of different devices: /device:TPU:27 before, /device:TPU:31 now
where the time goes in v3:
time: 64.2 us; the launch traced here: 63.5 us
  Pallas kernels  33.8 us (53%)
  starting transfers between devices  16.1 us (25%)
  waiting for transfers between devices  13.2 us (21%)
    ppermute x9, starting transfers between devices, permute(): return lax.ppermute(block, AXES, pairs)  16.1 us
    pallas_call x2, Pallas kernels, add_part(): pl.pallas_call(kernel, out_shape=(ACC, TOT), in_specs=[SMEM] + [VMEM] * (...  15.8 us
    ppermute x9, waiting for transfers between devices, permute(): return lax.ppermute(block, AXES, pairs)  13.2 us
    pallas_call x1, Pallas kernels, last_part(): pl.pallas_call(last_kernel, out_shape=jax.ShapeDtypeStruct(shape, BF16),...  11.8 us
    pallas_call x1, Pallas kernels, own_part(): pl.pallas_call(own_kernel, out_shape=(QT, ACC, TOT, pltpu.VMEM((1, M), jn...  5.25 us
  transfers between devices with their start and end apart: 9, of which 2 were waited for; matrix products, arithmetic and copies ran while one was open for 0% of the time, Pallas kernels for 33%

profile of v3, /device:TPU:31, one launch (start us, length us, event | category | flops | bytes accessed | tf_op | source)
XLA Modules:
  0.0 63.5 jit_solution(11377055004753534654)
XLA Ops:
  0.0 0.9 %pack.1.kv_ref.own = bf16[640,128]{1,0:T(8,128)(2,1)S(1)} custom-call(bf16[320,128]{1,0:T(8,128)(2,1)} %k_hbm.1, bf16[320,128]{1,0:T(8,128)(2,1)} %v_hbm.1), custom_call_target="tpu_custom_call" | custom-call | tf_op jit(solution)/shard_map/pack/pallas_call | solution.py:286
  1.0 3.5 %collective-permute-start = (bf16[640,128]{1,0:T(8,128)(2,1)S(1)}, bf16[640,128]{1,0:T(8,128)(2,1)S(1)}, u32[]{:S(2)}, u32[]{:S(2)}) collective-permute-start(bf16[640,128]{1,0:T(8,128)(2,1)S(1)} %pack.1.kv_ref.own), channel_id=1, source_target_pairs={{0,8},{1,9},{2,10},{3,11},{4,12},{5,13},{6,14},{7,15},{8,16},{9,17... | collective-permute-start | bytes 491528 | tf_op jit(solution)/shard_map/ppermute | solution.py:274
  4.5 6.2 %collective-permute-done.z = bf16[640,128]{1,0:T(8,128)(2,1)S(1)} collective-permute-done((bf16[640,128]{1,0:T(8,128)(2,1)S(1)}, bf16[640,128]{1,0:T(8,128)(2,1)S(1)}, u32[]{:S(2)}, u32[]{:S(2)}) %collective-permute-start) | collective-permute-done | bytes 163872 | tf_op jit(solution)/shard_map/ppermute | solution.py:274
  10.8 0.3 collective-permute-start.2
  11.0 1.3 %collective-permute-start.4 = (bf16[640,128]{1,0:T(8,128)(2,1)S(1)}, bf16[640,128]{1,0:T(8,128)(2,1)S(1)}, u32[]{:S(2)}, u32[]{:S(2)}) collective-permute-start(bf16[640,128]{1,0:T(8,128)(2,1)S(1)} %get-tuple-element.34), channel_id=1, source_target_pairs={{0,6},{1,7},{2,0},{3,1},{4,2},{5,3},{6,4},{7,5},{8,14},{9,15},{10,... | collective-permute-start | bytes 491528 | tf_op jit(solution)/shard_map/ppermute | solution.py:274
  12.3 1.1 %collective-permute-start.3 = (bf16[640,128]{1,0:T(8,128)(2,1)S(1)}, bf16[640,128]{1,0:T(8,128)(2,1)S(1)}, u32[]{:S(2)}, u32[]{:S(2)}) collective-permute-start(bf16[640,128]{1,0:T(8,128)(2,1)S(1)} %get-tuple-element.35), channel_id=1, source_target_pairs={{0,4},{1,5},{2,6},{3,7},{4,0},{5,1},{6,2},{7,3},{8,12},{9,13},{10,... | collective-permute-start | bytes 491528 | tf_op jit(solution)/shard_map/ppermute | solution.py:274
  13.4 5.0 %collective-permute-start.1 = (bf16[640,128]{1,0:T(8,128)(2,1)S(1)}, bf16[640,128]{1,0:T(8,128)(2,1)S(1)}, u32[]{:S(2)}, u32[]{:S(2)}) collective-permute-start(bf16[640,128]{1,0:T(8,128)(2,1)S(1)} %pack.1.kv_ref.own), channel_id=1, source_target_pairs={{0,1},{2,3},{4,5},{6,7},{8,9},{10,11},{12,13},{14,15},{16,17},{18,... | collective-permute-start | bytes 491528 | tf_op jit(solution)/shard_map/ppermute | solution.py:274
  18.4 0.1 collective-permute-start.8
  18.5 5.2 %own.1 = (bf16[256,5120]{1,0:T(8,128)(2,1)S(1)}, f32[128,5120]{1,0:T(8,128)S(1)}, f32[8,5120]{1,0:T(8,128)S(1)}, s32[1,1280]{1,0:T(1,128)S(1)}, s32[1]{0:T(128)}) custom-call(s32[64]{0:T(128)} %docs_hbm.1, bf16[320,2048]{1,0:T(8,128)(2,1)} %q_hbm.1, bf16[640,128]{1,0:T(8,128)(2,1)S(1)} %pack.1.kv_ref.own), custom_call_target="tpu_custom_call" | custom-call | flops 1677721600 | bytes 1048576 | tf_op jit(solution)/shard_map/own/pallas_call | solution.py:298
  23.7 0.0 collective-permute-done.2
  23.7 0.0 collective-permute-done.4
  23.8 0.0 collective-permute-done.3
  23.8 2.7 %collective-permute-start.5 = (bf16[1920,128]{1,0:T(8,128)(2,1)S(1)}, bf16[1920,128]{1,0:T(8,128)(2,1)S(1)}, u32[]{:S(2)}, u32[]{:S(2)}) collective-permute-start(bf16[1920,128]{1,0:T(8,128)(2,1)S(1)} %pad_maximum_fusion.near), channel_id=1, source_target_pairs={{0,8},{1,9},{2,10},{3,11},{4,12},{5,13},{6,14},{7,15},{8,16},{9,17... | collective-permute-start | bytes 1474568 | tf_op jit(solution)/shard_map/ppermute | solution.py:274
  26.5 0.8 %collective-permute-start.7 = (bf16[1920,128]{1,0:T(8,128)(2,1)S(1)}, bf16[1920,128]{1,0:T(8,128)(2,1)S(1)}, u32[]{:S(2)}, u32[]{:S(2)}) collective-permute-start(bf16[1920,128]{1,0:T(8,128)(2,1)S(1)} %pad_maximum_fusion.near), channel_id=1, source_target_pairs={{0,1},{1,0},{2,3},{3,2},{4,5},{5,4},{6,7},{7,6},{8,9},{9,8},{10,11... | collective-permute-start | bytes 1474568 | tf_op jit(solution)/shard_map/ppermute | solution.py:274
  27.3 0.0 collective-permute-done.1.x_ref
  27.3 0.0 collective-permute-done.8.z2
  27.3 5.7 %zpart.1 = (f32[128,5120]{1,0:T(8,128)S(1)}, f32[8,5120]{1,0:T(8,128)S(1)}) custom-call(s32[1]{0:T(128)} %get-tuple-element.20.first_ref, bf16[256,5120]{1,0:T(8,128)(2,1)S(1)} %get-tuple-element.21.qt_ref, bf16[640,128]{1,0:T(8,128)(2,1)S(1)} %collective-permute-done.z, ...), custom_call_target="tpu_custom_call", output_to_operand_aliasing={{0}: (5, {}), {1}: (6, {})} | custom-call | flops 5033164800 | bytes 1048576 | tf_op jit(solution)/shard_map/zpart/pallas_call | solution.py:320
  33.1 7.0 %collective-permute-done.5.far = bf16[1920,128]{1,0:T(8,128)(2,1)S(1)} collective-permute-done((bf16[1920,128]{1,0:T(8,128)(2,1)S(1)}, bf16[1920,128]{1,0:T(8,128)(2,1)S(1)}, u32[]{:S(2)}, u32[]{:S(2)}) %collective-permute-start.5) | collective-permute-done | bytes 491552 | tf_op jit(solution)/shard_map/ppermute | solution.py:274
  40.1 1.3 %collective-permute-start.6 = (bf16[1920,128]{1,0:T(8,128)(2,1)S(1)}, bf16[1920,128]{1,0:T(8,128)(2,1)S(1)}, u32[]{:S(2)}, u32[]{:S(2)}) collective-permute-start(bf16[1920,128]{1,0:T(8,128)(2,1)S(1)} %collective-permute-done.5.far), channel_id=1, source_target_pairs={{0,1},{1,0},{2,3},{3,2},{4,5},{5,4},{6,7},{7,6},{8,9},{9,8},{10,11... | collective-permute-start | bytes 1474568 | tf_op jit(solution)/shard_map/ppermute | solution.py:274
  41.5 0.0 collective-permute-done.7.near2
  41.5 10.0 %nearpart.1 = (f32[128,5120]{1,0:T(8,128)S(1)}, f32[8,5120]{1,0:T(8,128)S(1)}) custom-call(s32[1]{0:T(128)} %get-tuple-element.20.first_ref, bf16[256,5120]{1,0:T(8,128)(2,1)S(1)} %get-tuple-element.21.qt_ref, bf16[1920,128]{1,0:T(8,128)(2,1)S(1)} %pad_maximum_fusion.near, ...), custom_call_target="tpu_custom_call", output_to_operand_aliasing={{0}: (4, {}), {1}: (5, {})} | custom-call | flops 10066329600 | bytes 1048576 | tf_op jit(solution)/shard_map/nearpart/pallas_call | solution.py:320
  51.5 0.0 collective-permute-done.6.far2
  51.5 11.8 %last.1 = bf16[320,2048]{1,0:T(8,128)(2,1)} custom-call(s32[1]{0:T(128)} %get-tuple-element.20.first_ref, bf16[256,5120]{1,0:T(8,128)(2,1)S(1)} %get-tuple-element.21.qt_ref, bf16[640,128]{1,0:T(8,128)(2,1)S(1)} %collective-permute-done.1.x_ref, bf16[1920,128]{1,0:T(8,128)(2,1)S(1)} %collective-permute-done.5.far, ...), custom_call_target="tpu_custom_call" | custom-call | flops 10066329600 | bytes 1048576 | tf_op jit(solution)/shard_map/last/pallas_call | solution.py:334
  (2 shorter events, 0.1 us)
Async XLA Ops:
  1.0 9.8 %collective-permute-start = (bf16[640,128]{1,0:T(8,128)(2,1)S(1)}, bf16[640,128]{1,0:T(8,128)(2,1)S(1)}, u32[]{:S(2)}, u32[]{:S(2)}) collective-permute-start(bf16[640,128]{1,0:T(8,128)(2,1)S(1)} %pack.1.kv_ref.own), channel_id=1, source_target_pairs={{0,8},{1,9},{2,10},{3,11},{4,12},{5,13},{6,14},{7,15},{8,16},{9,17... | collective-permute-start | bytes 491528 | tf_op jit(solution)/shard_map/ppermute | solution.py:274
  10.8 13.0 %collective-permute-start.2 = (bf16[640,128]{1,0:T(8,128)(2,1)S(1)}, bf16[640,128]{1,0:T(8,128)(2,1)S(1)}, u32[]{:S(2)}, u32[]{:S(2)}) collective-permute-start(bf16[640,128]{1,0:T(8,128)(2,1)S(1)} %get-tuple-element.33), channel_id=1, source_target_pairs={{0,2},{1,3},{2,4},{3,5},{4,6},{5,7},{6,0},{7,1},{8,10},{9,11},{10,... | collective-permute-start | bytes 491528 | tf_op jit(solution)/shard_map/ppermute | solution.py:274
  11.0 12.7 %collective-permute-start.4 = (bf16[640,128]{1,0:T(8,128)(2,1)S(1)}, bf16[640,128]{1,0:T(8,128)(2,1)S(1)}, u32[]{:S(2)}, u32[]{:S(2)}) collective-permute-start(bf16[640,128]{1,0:T(8,128)(2,1)S(1)} %get-tuple-element.34), channel_id=1, source_target_pairs={{0,6},{1,7},{2,0},{3,1},{4,2},{5,3},{6,4},{7,5},{8,14},{9,15},{10,... | collective-permute-start | bytes 491528 | tf_op jit(solution)/shard_map/ppermute | solution.py:274
  12.3 11.5 %collective-permute-start.3 = (bf16[640,128]{1,0:T(8,128)(2,1)S(1)}, bf16[640,128]{1,0:T(8,128)(2,1)S(1)}, u32[]{:S(2)}, u32[]{:S(2)}) collective-permute-start(bf16[640,128]{1,0:T(8,128)(2,1)S(1)} %get-tuple-element.35), channel_id=1, source_target_pairs={{0,4},{1,5},{2,6},{3,7},{4,0},{5,1},{6,2},{7,3},{8,12},{9,13},{10,... | collective-permute-start | bytes 491528 | tf_op jit(solution)/shard_map/ppermute | solution.py:274
  13.4 13.9 %collective-permute-start.1 = (bf16[640,128]{1,0:T(8,128)(2,1)S(1)}, bf16[640,128]{1,0:T(8,128)(2,1)S(1)}, u32[]{:S(2)}, u32[]{:S(2)}) collective-permute-start(bf16[640,128]{1,0:T(8,128)(2,1)S(1)} %pack.1.kv_ref.own), channel_id=1, source_target_pairs={{0,1},{2,3},{4,5},{6,7},{8,9},{10,11},{12,13},{14,15},{16,17},{18,... | collective-permute-start | bytes 491528 | tf_op jit(solution)/shard_map/ppermute | solution.py:274
  18.4 8.9 %collective-permute-start.8 = (bf16[640,128]{1,0:T(8,128)(2,1)S(1)}, bf16[640,128]{1,0:T(8,128)(2,1)S(1)}, u32[]{:S(2)}, u32[]{:S(2)}) collective-permute-start(bf16[640,128]{1,0:T(8,128)(2,1)S(1)} %collective-permute-done.z), channel_id=1, source_target_pairs={{0,1},{1,0},{2,3},{3,2},{4,5},{5,4},{6,7},{7,6},{8,9},{9,8},{10,11... | collective-permute-start | bytes 491528 | tf_op jit(solution)/shard_map/ppermute | solution.py:274
  23.8 16.3 %collective-permute-start.5 = (bf16[1920,128]{1,0:T(8,128)(2,1)S(1)}, bf16[1920,128]{1,0:T(8,128)(2,1)S(1)}, u32[]{:S(2)}, u32[]{:S(2)}) collective-permute-start(bf16[1920,128]{1,0:T(8,128)(2,1)S(1)} %pad_maximum_fusion.near), channel_id=1, source_target_pairs={{0,8},{1,9},{2,10},{3,11},{4,12},{5,13},{6,14},{7,15},{8,16},{9,17... | collective-permute-start | bytes 1474568 | tf_op jit(solution)/shard_map/ppermute | solution.py:274
  26.5 15.0 %collective-permute-start.7 = (bf16[1920,128]{1,0:T(8,128)(2,1)S(1)}, bf16[1920,128]{1,0:T(8,128)(2,1)S(1)}, u32[]{:S(2)}, u32[]{:S(2)}) collective-permute-start(bf16[1920,128]{1,0:T(8,128)(2,1)S(1)} %pad_maximum_fusion.near), channel_id=1, source_target_pairs={{0,1},{1,0},{2,3},{3,2},{4,5},{5,4},{6,7},{7,6},{8,9},{9,8},{10,11... | collective-permute-start | bytes 1474568 | tf_op jit(solution)/shard_map/ppermute | solution.py:274
  40.1 11.4 %collective-permute-start.6 = (bf16[1920,128]{1,0:T(8,128)(2,1)S(1)}, bf16[1920,128]{1,0:T(8,128)(2,1)S(1)}, u32[]{:S(2)}, u32[]{:S(2)}) collective-permute-start(bf16[1920,128]{1,0:T(8,128)(2,1)S(1)} %collective-permute-done.5.far), channel_id=1, source_target_pairs={{0,1},{1,0},{2,3},{3,2},{4,5},{5,4},{6,7},{7,6},{8,9},{9,8},{10,11... | collective-permute-start | bytes 1474568 | tf_op jit(solution)/shard_map/ppermute | solution.py:274
